TPU v7x, 512 devices: a whole 4x4x16 slice. The times are simulated.
512 devices in a mesh: row: 16 (over z_lo, core), col: 32 (over y, x, z_hi).
Axes of the slice: x: 4, y: 4, z: 16 (z_hi: 2, z_lo: 8; z = z_hi * 8 + z_lo), core: 2. Of those that a mesh axis runs over, the one named last changes fastest.
Arguments:
- activations: bfloat16 [1024, 5120], P('col', 'row'), may hold values from -1.5 to 1.5
- grad_output: bfloat16 [1024, 5120], P('col', 'row'), may hold values from -1.5 to 1.5
- gate_pre: bfloat16 [1024, 25600], P('row', 'col'), may hold values from -6 to 6
- up_pre: bfloat16 [1024, 25600], P('row', 'col'), may hold values from -6 to 6
- gate_weight: bfloat16 [5120, 25600], P('row', 'col'), may hold values from -0.078125 to 0.078125
- up_weight: bfloat16 [5120, 25600], P('row', 'col'), may hold values from -0.078125 to 0.078125
- down_weight: bfloat16 [25600, 5120], P('col', 'row'), may hold values from -0.0390625 to 0.0390625
Outputs:
- grad_input: float32 [1024, 5120], P('col', 'row')
- grad_gate_weight: float32 [5120, 25600], P('row', 'col')
- grad_up_weight: float32 [5120, 25600], P('row', 'col')
- grad_down_weight: float32 [25600, 5120], P('col', 'row')
All inputs are finite; a program needn't handle non-finite values.
Results may differ from a plain program's by a relative error of at most 0.0029.
Values may be sent and summed in bfloat16 or wider, within the bound.
No kernel may reach another device: no remote copies, remote signals or barrier semaphores. Data moves between devices by JAX's collectives and lax.ppermute only.
A program may use at most 64 MiB of HBM per device.

v0:
```python
import jax
import jax.numpy as jnp
from jax import lax
from jax.sharding import PartitionSpec as P


def swiglu_back(gate_vals, up_vals, grad_hidden):
    gate_wide = gate_vals.astype(jnp.float32)
    up_wide = up_vals.astype(jnp.float32)
    logistic = jax.nn.sigmoid(gate_wide)
    silu_val = gate_wide * logistic
    hidden = (silu_val * up_wide).astype(jnp.bfloat16)
    grad_gate = (grad_hidden * up_wide * logistic * (1.0 + gate_wide * (1.0 - logistic))).astype(
        jnp.bfloat16
    )
    grad_up = (grad_hidden * silu_val).astype(jnp.bfloat16)
    return (hidden, grad_gate, grad_up)


def right_trans(left, right):
    return lax.dot_general(
        left, right, (((1,), (1,)), ((), ())), preferred_element_type=jnp.float32
    )


def left_trans(left, right):
    return lax.dot_general(
        left, right, (((0,), (0,)), ((), ())), preferred_element_type=jnp.float32
    )


def shards(activations, grad_output, gate_pre, up_pre, gate_weight, up_weight, down_weight):
    grad_rows = lax.all_gather(grad_output, "col", axis=0, tiled=True)
    segment = grad_rows
    own_hidden = lax.psum_scatter(
        right_trans(segment, down_weight), "row", scatter_dimension=0, tiled=True
    )
    local_h, local_gate, local_up = swiglu_back(gate_pre, up_pre, own_hidden)
    hidden, grad_gate, grad_up = (
        lax.all_gather(local_h, "row", axis=0, tiled=True),
        lax.all_gather(local_gate, "row", axis=0, tiled=True),
        lax.all_gather(local_up, "row", axis=0, tiled=True),
    )
    grad_down_weight = left_trans(hidden, grad_rows)
    segment = lax.all_gather(activations, "col", axis=0, tiled=True)
    gate_slice = grad_gate
    up_slice = grad_up
    grad_gate_weight = left_trans(segment, gate_slice)
    grad_up_weight = left_trans(segment, up_slice)
    gate_slice = grad_gate
    up_slice = grad_up
    grad_input = lax.psum_scatter(
        right_trans(gate_slice, gate_weight) + right_trans(up_slice, up_weight),
        "col",
        scatter_dimension=0,
        tiled=True,
    )
    return (grad_input, grad_gate_weight, grad_up_weight, grad_down_weight)


def solution(mesh):
    placed = (
        P("col", "row"),
        P("col", "row"),
        P("row", "col"),
        P("row", "col"),
        P("row", "col"),
        P("row", "col"),
        P("col", "row"),
    )
    return jax.shard_map(
        shards,
        mesh=mesh,
        in_specs=placed,
        out_specs=(P("col", "row"), P("row", "col"), P("row", "col"), P("col", "row")),
        check_vma=False,
    )
```

profile of v0, /device:TPU:4, one launch (start us, length us, event | category | flops | bytes accessed | tf_op | source)
XLA Modules:
  0.0 963.3 jit_solution(5049619266917806084)
XLA Ops:
  7.2 0.0 copy-start
  7.2 0.0 reduce-scatter.3.cloned.1.call-start
  7.2 202.3 %all_gather.15 = bf16[1024,320]{1,0:T(8,128)(2,1)S(1)} all-gather(bf16[32,320]{1,0:T(8,128)(2,1)} %param.8), channel_id=1, replica_groups=mesh['row'=16,'col'=32] {'col'}, dimensions={0}, use_global_device_ids=true | all-gather | bytes 675840 | tf_op jit(solution)/shard_map/all_gather | solution.py:33
  209.5 3.0 fusion.8
  212.4 0.0 reduce-scatter.3.cloned.1.call-update
  212.5 0.0 all-gather.4.cloned.1.call-start
  212.5 108.8 %reduce-scatter.3.cloned.1.call-done = f32[64,800]{1,0:T(8,128)} async-done(((f32[1024,800]{1,0:T(8,128)}), f32[64,800]{1,0:T(8,128)}) %reduce-scatter.3.cloned.1.call-update) | async-done | bytes 204816 | tf_op jit(solution)/shard_map/reduce_scatter | solution.py:35
  321.3 1.8 multiply_convert_fusion
  323.1 0.0 all-gather.4.cloned.1.call-update
  323.1 0.0 all-gather.6.cloned.1.call-start
  323.2 0.7 all-gather.6.cloned.1.call-update
  323.9 0.0 all-gather.8.cloned.1.call-start
  323.9 0.5 all-gather.8.cloned.1.call-update
  324.5 0.0 reduce-scatter.5.cloned.1.call-start
  324.5 94.3 %all-gather.4.cloned.1.call-done = bf16[1024,800]{1,0:T(8,128)(2,1)} async-done(((bf16[64,800]{1,0:T(8,128)(2,1)}), bf16[1024,800]{1,0:T(8,128)(2,1)}) %all-gather.4.cloned.1.call-update) | async-done | bytes 1638416 | tf_op jit(solution)/shard_map/all_gather | solution.py:41
  418.8 2.8 fusion.9
  421.6 100.9 %all-gather.6.cloned.1.call-done = bf16[1024,800]{1,0:T(8,128)(2,1)} async-done(((bf16[64,800]{1,0:T(8,128)(2,1)}), bf16[1024,800]{1,0:T(8,128)(2,1)}) %all-gather.6.cloned.1.call-update) | async-done | bytes 1638416 | tf_op jit(solution)/shard_map/all_gather | solution.py:42
  522.5 3.9 convolution_add_fusion
  526.4 0.0 reduce-scatter.5.cloned.1.call-update
  526.5 195.2 %all_gather.18 = bf16[1024,320]{1,0:T(8,128)(2,1)S(1)} all-gather(bf16[32,320]{1,0:T(8,128)(2,1)S(1)} %copy-done.5), channel_id=1, replica_groups=mesh['row'=16,'col'=32] {'col'}, dimensions={0}, use_global_device_ids=true | all-gather | bytes 675840 | tf_op jit(solution)/shard_map/all_gather | solution.py:45
  721.7 1.9 convolution_bitcast_fusion
  723.6 1.9 convolution_bitcast_fusion.1
  725.5 3.4 fusion.10
  728.9 227.9 %reduce-scatter.5.cloned.1.call-done = f32[32,320]{1,0:T(8,128)} async-done(((f32[1024,320]{1,0:T(8,128)}), f32[32,320]{1,0:T(8,128)}) %reduce-scatter.5.cloned.1.call-update) | async-done | bytes 40976 | tf_op jit(solution)/shard_map/reduce_scatter | solution.py:52
  (14 shorter events, 0.0 us)
Async XLA Ops:
  7.2 202.3 %copy-start = (bf16[800,320]{0,1:T(8,128)(2,1)S(1)}, bf16[800,320]{0,1:T(8,128)(2,1)}, u32[]{:S(2)}) copy-start(bf16[800,320]{0,1:T(8,128)(2,1)} %param.13) | copy-start | bytes 1536004
  7.2 314.2 %reduce-scatter.3.cloned.1.call-start = ((), (), s32[]{:S(2)}) async-start(), calls=%async_computation.2 | async-start | bytes 3899392 | tf_op jit(solution)/shard_map/reduce_scatter | solution.py:35
  212.4 108.9 %copy-start.3 = (bf16[64,800]{1,0:T(8,128)(2,1)S(1)}, bf16[64,800]{1,0:T(8,128)(2,1)}, u32[]{:S(2)}) copy-start(bf16[64,800]{1,0:T(8,128)(2,1)} %param.9) | copy-start | bytes 307204
  212.4 108.9 %copy-start.4 = (bf16[64,800]{1,0:T(8,128)(2,1)S(1)}, bf16[64,800]{1,0:T(8,128)(2,1)}, u32[]{:S(2)}) copy-start(bf16[64,800]{1,0:T(8,128)(2,1)} %param.10) | copy-start | bytes 307204
  212.5 206.4 %all-gather.4.cloned.1.call-start = ((), (), s32[]{:S(2)}) async-start(), calls=%async_computation.3 | async-start | bytes 1949696 | tf_op jit(solution)/shard_map/all_gather | solution.py:41
  323.1 199.4 %all-gather.6.cloned.1.call-start = ((), (), s32[]{:S(2)}) async-start(), calls=%async_computation.4 | async-start | bytes 1949696 | tf_op jit(solution)/shard_map/all_gather | solution.py:42
  323.9 401.6 %all-gather.8.cloned.1.call-start = ((), (), s32[]{:S(2)}) async-start(), calls=%async_computation.6 | async-start | bytes 1949696 | tf_op jit(solution)/shard_map/all_gather | solution.py:40
  324.5 198.1 %copy-start.2 = (bf16[320,800]{1,0:T(8,128)(2,1)S(1)}, bf16[320,800]{1,0:T(8,128)(2,1)}, u32[]{:S(2)}) copy-start(bf16[320,800]{1,0:T(8,128)(2,1)} %param.12) | copy-start | bytes 1536004
  324.5 632.3 %reduce-scatter.5.cloned.1.call-start = ((), (), s32[]{:S(2)}) async-start(), calls=%async_computation.5 | async-start | bytes 1622016 | tf_op jit(solution)/shard_map/reduce_scatter | solution.py:52
  421.6 104.8 %copy-start.5 = (bf16[32,320]{1,0:T(8,128)(2,1)S(1)}, bf16[32,320]{1,0:T(8,128)(2,1)}, u32[]{:S(2)}) copy-start(bf16[32,320]{1,0:T(8,128)(2,1)} %param.7) | copy-start | bytes 61444
  526.4 195.3 %copy-start.1 = (bf16[1024,800]{1,0:T(8,128)(2,1)S(1)}, bf16[1024,800]{1,0:T(8,128)(2,1)}, u32[]{:S(2)}) copy-start(bf16[1024,800]{1,0:T(8,128)(2,1)} %all-gather.6.cloned.1.call-done) | copy-start | bytes 4915204
  721.7 1.9 copy-start.6
Sparse Core Ops, SparseCore 0:
  212.6 108.6 reduce-scatter.2
  324.0 94.7 all-gather.3
  421.5 100.9 all-gather.5
  524.5 108.4 all-gather.7
  639.6 317.1 reduce-scatter.4
where the time goes:
time: 964 us; the launch traced here: 963 us
  waiting for transfers between devices  533 us (55%)
  blocking collectives  397 us (41%)
  matrix products  16.9 us (2%)
  between operations  13.8 us (1%)
    reduce_scatter x1, waiting for transfers between devices, shards(): lax.psum_scatter(right_trans(gate_slice, gate_weight) + right_trans(up_sl...  228 us
    all_gather x1, blocking collectives, shards(): grad_rows = lax.all_gather(grad_output, 'col', axis=0, tiled=True)  202 us
    all_gather x1, blocking collectives, shards(): segment = lax.all_gather(activations, 'col', axis=0, tiled=True)  195 us
    reduce_scatter x1, waiting for transfers between devices, shards(): lax.psum_scatter(right_trans(segment, down_weight), 'row', scatter_dimens...  109 us
    all_gather x1, waiting for transfers between devices, shards(): lax.all_gather(local_up, 'row', axis=0, tiled=True)  101 us
    all_gather x1, waiting for transfers between devices, shards(): lax.all_gather(local_gate, 'row', axis=0, tiled=True)  94.3 us
  transfers between devices with their start and end apart: 5, of which 4 were waited for; matrix products, arithmetic and copies ran while one was open for 1% of the time, Pallas kernels for 0%

commit v1 on v0

v1 whole, which is shorter than its diff:
```python
import jax
import jax.numpy as jnp
from jax import lax
from jax.sharding import Mesh
from jax.sharding import PartitionSpec as P

F32, F16, BF16 = jnp.float32, jnp.float16, jnp.bfloat16

SIZES = dict(p=2, q=2, r=2, c=2, y=4, v=2, w=2, h=2)
ROW, COL = ("p", "q", "r", "c"), ("y", "v", "w", "h")
LINE, QUAD, PLANE = ("p", "q", "r"), ("q", "r"), ("w", "y", "v")


def swap(x, axis):
    return lax.ppermute(x, axis, [(0, 1), (1, 0)])


def halves(x, at):
    n = x.shape[0] // 2
    return (
        lax.dynamic_slice_in_dim(x, at * n, n, 0),
        lax.dynamic_slice_in_dim(x, (1 - at) * n, n, 0),
    )


def right_trans(left, right):
    return lax.dot_general(left, right, (((1,), (1,)), ((), ())), preferred_element_type=F32)


def left_trans(left, right):
    return lax.dot_general(left, right, (((0,), (0,)), ((), ())), preferred_element_type=F32)


def encode(x, bound):
    power = jnp.clip(14.0 - jnp.ceil(jnp.log2(bound)), -100.0, 100.0)
    tail = jnp.full(x.shape[:-1] + (1,), power, F32)
    return jnp.concatenate([x * jnp.exp2(power), tail], axis=-1).astype(F16)


def decode(coded):
    wide = coded.astype(F32)
    return wide[..., :-1] * jnp.exp2(-wide[..., -1:])


def bound_of(coded):
    return jnp.exp2(15.0 - coded[..., 0, -1].astype(F32))


def plane_gather(x):
    got = lax.all_to_all(jnp.broadcast_to(x[None], (16,) + x.shape), PLANE, 0, 0, tiled=True)
    return got.reshape((16 * x.shape[0],) + x.shape[1:])


def shards(activations, grad_output, gate_pre, up_pre, gate_weight, up_weight, down_weight):
    core, run = lax.axis_index("c"), lax.axis_index("h")

    saved = lax.all_gather(jnp.stack([gate_pre, up_pre]), LINE, axis=1, tiled=True)
    saved_other = swap(saved, "c")

    pair = lax.all_gather(jnp.stack([grad_output, activations]), "h", axis=1, tiled=True)
    grad_rows = plane_gather(pair[0])
    act_rows = plane_gather(pair[1])
    down_other = swap(down_weight, "c")

    mine, theirs = halves(grad_rows, core)
    given = swap(theirs, "c")
    part = right_trans(mine, down_weight) + right_trans(given, down_other)
    top = jnp.maximum(jnp.max(jnp.abs(grad_rows)), jnp.max(jnp.abs(given))).astype(F32)
    heavy = jnp.maximum(jnp.max(jnp.abs(down_weight)), jnp.max(jnp.abs(down_other))).astype(F32)
    bound = 2.0 * down_weight.shape[1] * top * heavy

    coded = encode(part, bound).reshape(4, 128, -1)
    coded = lax.all_to_all(coded, QUAD, 0, 0, tiled=True)
    part = jnp.sum(decode(coded), axis=0)
    bound = jnp.sum(bound_of(coded))
    coded = encode(part, bound)
    far = swap(coded, "p")
    part = decode(coded) + decode(far)
    bound = bound_of(coded) + bound_of(far)
    coded = lax.all_gather(encode(part, bound), QUAD, axis=0, tiled=True)
    coded_other = swap(coded, "c")

    def by_core(own, other):
        first = jnp.where(core == 0, own, other)
        second = jnp.where(core == 0, other, own)
        return jnp.concatenate([first, second], axis=0)

    gate_wide = by_core(saved[0], saved_other[0]).astype(F32)
    up_wide = by_core(saved[1], saved_other[1]).astype(F32)
    logistic = jax.nn.sigmoid(gate_wide)
    silu_val = gate_wide * logistic
    hidden = (silu_val * up_wide).astype(BF16)
    gate_slope = up_wide * logistic * (1.0 + gate_wide * (1.0 - logistic))

    grad_down_weight = left_trans(hidden, grad_rows)

    grad_hidden = by_core(decode(coded), decode(coded_other))
    grad_gate = (grad_hidden * gate_slope).astype(BF16)
    grad_up = (grad_hidden * silu_val).astype(BF16)

    share = right_trans(grad_gate, gate_weight) + right_trans(grad_up, up_weight)
    share = lax.all_to_all(share.astype(BF16).reshape(16, 64, -1), PLANE, 0, 0, tiled=True)
    share = jnp.sum(share.astype(F32), axis=0)
    near, away = halves(share, run)
    grad_input = near + swap(away, "h")

    grad_gate_weight = left_trans(act_rows, grad_gate)
    grad_up_weight = left_trans(act_rows, grad_up)
    return (grad_input, grad_gate_weight, grad_up_weight, grad_down_weight)


def solution(mesh):
    fine = Mesh(mesh.devices.reshape(tuple(SIZES.values())), tuple(SIZES))
    wide, units, down = P(COL, ROW), P(ROW, COL), P(COL, ROW)
    return jax.shard_map(
        shards,
        mesh=fine,
        in_specs=(wide, wide, units, units, units, units, down),
        out_specs=(wide, units, units, down),
        check_vma=False,
    )
```

time: 964 us -> 242 us (0.25)
  waiting for transfers between devices: 533 us -> 96 us
  blocking collectives: 397 us -> 35.7 us
  starting transfers between devices: 0.2 us -> 45.2 us
  local copies, waits for them, and re-layouts: 0.04 us -> 14.5 us
  other arithmetic: 1.78 us -> 15 us
    all_gather x2, blocking collectives: 397 us -> 35.7 us  [the longest x1 18.5 us: shards(): coded = lax.all_gather(encode(part, bound), QUAD, axis=0, tiled=True)]
    reduce_scatter x2 -> x0, waiting for transfers between devices: 337 us -> none  [the longest x1 228 us: shards(): lax.psum_scatter(right_trans(gate_slice, gate_weight) + right_trans(up_sl...]
    all_gather x3 -> x1, waiting for transfers between devices: 195 us -> 55.9 us  [shards(): lax.all_gather(jnp.stack([gate_pre, up_pre]), LINE, axis=1, tiled=True)]
    all_to_all x0 -> x4, starting transfers between devices: none -> 26.3 us  [the longest x2 16.8 us: plane_gather(): lax.all_to_all(jnp.broadcast_to(x[None], (16,) + x.shape), PLANE, 0, 0, t...]
    ppermute x0 -> x6, waiting for transfers between devices: none -> 23.1 us  [swap(): return lax.ppermute(x, axis, [(0, 1), (1, 0)])]
    ppermute x0 -> x6, starting transfers between devices: none -> 18.9 us  [swap(): return lax.ppermute(x, axis, [(0, 1), (1, 0)])]
    all_to_all x0 -> x4, waiting for transfers between devices: none -> 17.1 us  [the longest x2 10.9 us: plane_gather(): lax.all_to_all(jnp.broadcast_to(x[None], (16,) + x.shape), PLANE, 0, 0, t...]
  transfers between devices with their start and end apart: 5 -> 11, of which waited for: 4 -> 6; matrix products, arithmetic and copies ran while one was open for 1% -> 18% of each run, Pallas kernels for 0% -> 0%
where the time goes in v1:
time: 242 us; the launch traced here: 240 us
  waiting for transfers between devices  96 us (40%)
  starting transfers between devices  45.2 us (19%)
  blocking collectives  35.7 us (15%)
  between operations  18.8 us (8%)
  matrix products  15.1 us (6%)
  other arithmetic  15 us (6%)
  local copies, waits for them, and re-layouts  14.5 us (6%)
    all_gather x1, waiting for transfers between devices, shards(): lax.all_gather(jnp.stack([gate_pre, up_pre]), LINE, axis=1, tiled=True)  55.9 us
    ppermute x6, waiting for transfers between devices, swap(): return lax.ppermute(x, axis, [(0, 1), (1, 0)])  23.1 us
    ppermute x6, starting transfers between devices, swap(): return lax.ppermute(x, axis, [(0, 1), (1, 0)])  18.9 us
    all_gather x1, blocking collectives, shards(): coded = lax.all_gather(encode(part, bound), QUAD, axis=0, tiled=True)  18.5 us
    all_gather x1, blocking collectives, shards(): lax.all_gather(jnp.stack([grad_output, activations]), 'h', axis=1, tiled=...  17.2 us
    all_to_all x2, starting transfers between devices, plane_gather(): lax.all_to_all(jnp.broadcast_to(x[None], (16,) + x.shape), PLANE, 0, 0, t...  16.8 us
    all_to_all x2, waiting for transfers between devices, plane_gather(): lax.all_to_all(jnp.broadcast_to(x[None], (16,) + x.shape), PLANE, 0, 0, t...  10.9 us
    dot_general x3, matrix products, left_trans(): lax.dot_general(left, right, (((0,), (0,)), ((), ())), preferred_element_...  9.95 us
  transfers between devices with their start and end apart: 11, of which 6 were waited for; matrix products, arithmetic and copies ran while one was open for 18% of the time, Pallas kernels for 0%

profile of v1, /device:TPU:4, one launch (start us, length us, event | category | flops | bytes accessed | tf_op | source)
XLA Modules:
  0.0 240.4 jit_solution(8857466810776819002)
XLA Ops:
  7.2 2.1 collective-permute-start.1
  10.0 17.2 %all_gather.9 = bf16[2,64,320]{2,1,0:T(8,128)(2,1)S(1)} all-gather(bf16[2,32,320]{2,1,0:T(8,128)(2,1)S(1)} %pad_maximum_fusion.6), channel_id=1, replica_groups=mesh['p'=2,'q'=2,'r'=2,'c'=2,'y'=4,'v'=2,'w'=2,'h'=2] {'h'}, dimensions={1}, use_global_device_ids=true | all-gather | bytes 122880 | tf_op jit(solution)/shard_map/all_gather | solution.py:60
  28.2 7.4 %all-to-all-start = ((bf16[16,64,320]{2,1,0:T(8,128)(2,1)}), bf16[16,64,320]{2,1,0:T(8,128)(2,1)S(1)}, u32[]{:S(2)}, u32[]{:S(2)}) async-start(bf16[16,64,320]{2,1,0:T(8,128)(2,1)} %broadcast_in_dim.18), calls=%async_computation | async-start | bytes 1572864 | tf_op jit(solution)/shard_map/all_to_all | solution.py:50
  39.5 8.2 %all-to-all-done = bf16[16,64,320]{2,1,0:T(8,128)(2,1)S(1)} async-done(((bf16[16,64,320]{2,1,0:T(8,128)(2,1)}), bf16[16,64,320]{2,1,0:T(8,128)(2,1)S(1)}, u32[]{:S(2)}, u32[]{:S(2)}) %all-to-all-start) | async-done | bytes 655392 | tf_op jit(solution)/shard_map/all_to_all | solution.py:50
  48.6 1.9 collective-permute-start
  55.1 1.7 multiply_convert_fusion.1
  58.8 4.2 %all-to-all-start.1 = ((f16[4,128,801]{1,2,0:T(8,128)(2,1)}), f16[4,128,801]{1,2,0:T(8,128)(2,1)}, u32[]{:S(2)}, u32[]{:S(2)}) async-start(f16[4,128,801]{1,2,0:T(8,128)(2,1)} %copy.47), calls=%async_computation.1 | async-start | bytes 1654784 | tf_op jit(solution)/shard_map/all_to_all | solution.py:73
  63.0 55.9 %all-gather.2.cloned.1.call-done = bf16[2,512,800]{2,0,1:T(2,128)(2,1)} async-done(((bf16[2,64,800]{2,0,1:T(2,128)(2,1)}), bf16[2,512,800]{2,0,1:T(2,128)(2,1)}) %all-gather.2.cloned.1.call-update) | async-done | bytes 1638416 | tf_op jit(solution)/shard_map/all_gather | solution.py:57
  118.9 4.6 %copy.51 = bf16[2,512,800]{1,2,0:T(8,128)(2,1)S(1)} copy(bf16[2,512,800]{2,0,1:T(2,128)(2,1)} %all-gather.2.cloned.1.call-done) | data formatting | bytes 3276800 | tf_op jit(solution)/shard_map/all_gather | solution.py:57
  123.5 1.9 collective-permute-start.4
  129.8 2.9 %collective-permute-start.2 = (f16[128,801]{0,1:T(8,128)(2,1)}, f16[128,801]{0,1:T(8,128)(2,1)}, u32[]{:S(2)}, u32[]{:S(2)}) collective-permute-start(f16[128,801]{0,1:T(8,128)(2,1)} %get-tuple-element.13), channel_id=1, source_target_pairs={{0,256},{256,0},{1,257},{257,1},{2,258},{258,2},{3,259},{259,3},{4... | collective-permute-start | bytes 615176 | tf_op jit(solution)/shard_map/ppermute | solution.py:15
  132.8 20.1 %collective-permute-done.2 = f16[128,801]{0,1:T(8,128)(2,1)} collective-permute-done((f16[128,801]{0,1:T(8,128)(2,1)}, f16[128,801]{0,1:T(8,128)(2,1)}, u32[]{:S(2)}, u32[]{:S(2)}) %collective-permute-start.2) | collective-permute-done | bytes 205088 | tf_op jit(solution)/shard_map/ppermute | solution.py:15
  156.0 18.5 %all_gather.10 = f16[512,801]{0,1:T(8,128)(2,1)} all-gather(f16[128,801]{0,1:T(8,128)(2,1)S(1)} %concatenate.20), channel_id=1, replica_groups=mesh['p'=2,'q'=2,'r'=2,'c'=2,'y'=4,'v'=2,'w'=2,'h'=2] {'q','r'}, dimensions={0}, use_global_device_ids=true | all-gather | bytes 1025280 | tf_op jit(solution)/shard_map/all_gather | solution.py:80
  174.5 1.9 collective-permute-start.3
  177.4 9.3 %all-to-all-start.3 = ((bf16[16,64,320]{2,1,0:T(8,128)(2,1)}), bf16[16,64,320]{2,1,0:T(8,128)(2,1)}, u32[]{:S(2)}, u32[]{:S(2)}) async-start(bf16[16,64,320]{2,1,0:T(8,128)(2,1)} %broadcast_in_dim.20), calls=%async_computation.3 | async-start | bytes 1572864 | tf_op jit(solution)/shard_map/all_to_all | solution.py:50
  191.8 1.8 fusion.2
  197.3 2.7 %all-to-all-done.3 = bf16[16,64,320]{2,1,0:T(8,128)(2,1)} async-done(((bf16[16,64,320]{2,1,0:T(8,128)(2,1)}), bf16[16,64,320]{2,1,0:T(8,128)(2,1)}, u32[]{:S(2)}, u32[]{:S(2)}) %all-to-all-start.3) | async-done | bytes 655392 | tf_op jit(solution)/shard_map/all_to_all | solution.py:50
  200.0 5.3 %all-to-all-start.2 = ((bf16[16,64,320]{2,1,0:T(8,128)(2,1)}), bf16[16,64,320]{2,1,0:T(8,128)(2,1)S(1)}, u32[]{:S(2)}, u32[]{:S(2)}) async-start(bf16[16,64,320]{2,1,0:T(8,128)(2,1)} %bitcast.18), calls=%async_computation.2 | async-start | bytes 1572864 | tf_op jit(solution)/shard_map/all_to_all | solution.py:102
  205.3 3.8 %fusion.34 = f32[320,800]{1,0:T(8,128)} fusion(bf16[1024,320]{1,0:T(8,128)(2,1)} %bitcast.20, bf16[1024,800]{0,1:T(8,128)(2,1)} %copy-done.12), kind=kOutput, calls=%fused_computation.73 | convolution fusion | flops 524288000 | bytes 3317760 | tf_op jit(solution)/shard_map/dot_general | solution.py:31
  209.2 2.4 fusion.8
  211.6 6.2 %all-to-all-done.2 = bf16[16,64,320]{2,1,0:T(8,128)(2,1)S(1)} async-done(((bf16[16,64,320]{2,1,0:T(8,128)(2,1)}), bf16[16,64,320]{2,1,0:T(8,128)(2,1)S(1)}, u32[]{:S(2)}, u32[]{:S(2)}) %all-to-all-start.2) | async-done | bytes 655392 | tf_op jit(solution)/shard_map/all_to_all | solution.py:102
  217.9 8.2 %collective-permute-start.5 = (f32[32,320]{1,0:T(8,128)S(1)}, f32[32,320]{1,0:T(8,128)S(1)}, u32[]{:S(2)}, u32[]{:S(2)}) collective-permute-start(f32[32,320]{1,0:T(8,128)S(1)} %constant_dynamic-slice_fusion), channel_id=1, source_target_pairs={{0,1},{1,0},{2,3},{3,2},{4,5},{5,4},{6,7},{7,6},{8,9},{9,8},{10,11... | collective-permute-start | bytes 122888 | tf_op jit(solution)/shard_map/ppermute | solution.py:15
  226.2 3.7 %fusion.35 = f32[320,800]{1,0:T(8,128)} fusion(bf16[1024,320]{1,0:T(8,128)(2,1)} %bitcast.20, bf16[1024,800]{0,1:T(8,128)(2,1)} %copy-done.11), kind=kOutput, calls=%fused_computation.74 | convolution fusion | flops 524288000 | bytes 3317760 | tf_op jit(solution)/shard_map/dot_general | solution.py:31
  229.9 3.0 %collective-permute-done.5 = f32[32,320]{1,0:T(8,128)S(1)} collective-permute-done((f32[32,320]{1,0:T(8,128)S(1)}, f32[32,320]{1,0:T(8,128)S(1)}, u32[]{:S(2)}, u32[]{:S(2)}) %collective-permute-start.5) | collective-permute-done | bytes 40992 | tf_op jit(solution)/shard_map/ppermute | solution.py:15
  (81 shorter events, 26.6 us)
Async XLA Ops:
  7.2 186.5 %copy-start = (bf16[320,800]{1,0:T(8,128)(2,1)S(1)}, bf16[320,800]{1,0:T(8,128)(2,1)}, u32[]{:S(2)}) copy-start(bf16[320,800]{1,0:T(8,128)(2,1)} %param.12) | copy-start | bytes 1536004
  7.2 28.5 %copy-start.14 = (bf16[64,800]{1,0:T(8,128)(2,1)S(1)}, bf16[64,800]{1,0:T(8,128)(2,1)}, u32[]{:S(2)}) copy-start(bf16[64,800]{1,0:T(8,128)(2,1)} %param.9) | copy-start | bytes 307204
  7.2 28.5 %copy-start.13 = (bf16[64,800]{1,0:T(8,128)(2,1)S(1)}, bf16[64,800]{1,0:T(8,128)(2,1)}, u32[]{:S(2)}) copy-start(bf16[64,800]{1,0:T(8,128)(2,1)} %param.10) | copy-start | bytes 307204
  7.2 30.2 %collective-permute-start.1 = (bf16[800,320]{0,1:T(8,128)(2,1)}, bf16[800,320]{0,1:T(8,128)(2,1)S(1)}, u32[]{:S(2)}, u32[]{:S(2)}) collective-permute-start(bf16[800,320]{0,1:T(8,128)(2,1)} %param.13), channel_id=1, source_target_pairs={{0,32},{32,0},{1,33},{33,1},{2,34},{34,2},{3,35},{35,3},{4,36},{36... | collective-permute-start | bytes 1536008 | tf_op jit(solution)/shard_map/ppermute | solution.py:15
  27.2 9.5 %copy-start.10 = (bf16[800,320]{0,1:T(8,128)(2,1)S(1)}, bf16[800,320]{0,1:T(8,128)(2,1)}, u32[]{:S(2)}) copy-start(bf16[800,320]{0,1:T(8,128)(2,1)} %param.13) | copy-start | bytes 1536004
  28.2 19.5 %all-to-all-start = ((bf16[16,64,320]{2,1,0:T(8,128)(2,1)}), bf16[16,64,320]{2,1,0:T(8,128)(2,1)S(1)}, u32[]{:S(2)}, u32[]{:S(2)}) async-start(bf16[16,64,320]{2,1,0:T(8,128)(2,1)} %broadcast_in_dim.18), calls=%async_computation | async-start | bytes 1572864 | tf_op jit(solution)/shard_map/all_to_all | solution.py:50
  35.7 83.2 %all-gather.2.cloned.1.call-start = ((), (), s32[]{:S(2)}) async-start(), calls=%async_computation.4 | async-start | bytes 2064384 | tf_op jit(solution)/shard_map/all_gather | solution.py:57
  37.4 13.1 %copy-start.9 = (bf16[800,320]{0,1:T(8,128)(2,1)}, bf16[800,320]{0,1:T(8,128)(2,1)S(1)}, u32[]{:S(2)}) copy-start(bf16[800,320]{0,1:T(8,128)(2,1)S(1)} %collective-permute-done.1) | copy-start | bytes 1536004
  48.6 4.4 %collective-permute-start = (bf16[512,320]{0,1:T(8,128)(2,1)}, bf16[512,320]{0,1:T(8,128)(2,1)S(1)}, u32[]{:S(2)}, u32[]{:S(2)}) collective-permute-start(bf16[512,320]{0,1:T(8,128)(2,1)} %copy.56), channel_id=1, source_target_pairs={{0,32},{32,0},{1,33},{33,1},{2,34},{34,2},{3,35},{35,3},{4,36},{36... | collective-permute-start | bytes 983048 | tf_op jit(solution)/shard_map/ppermute | solution.py:15
  58.8 66.7 %all-to-all-start.1 = ((f16[4,128,801]{1,2,0:T(8,128)(2,1)}), f16[4,128,801]{1,2,0:T(8,128)(2,1)}, u32[]{:S(2)}, u32[]{:S(2)}) async-start(f16[4,128,801]{1,2,0:T(8,128)(2,1)} %copy.47), calls=%async_computation.1 | async-start | bytes 1654784 | tf_op jit(solution)/shard_map/all_to_all | solution.py:73
  123.5 66.6 %collective-permute-start.4 = (bf16[2,512,800]{1,2,0:T(8,128)(2,1)S(1)}, bf16[2,512,800]{1,2,0:T(8,128)(2,1)}, u32[]{:S(2)}, u32[]{:S(2)}) collective-permute-start(bf16[2,512,800]{1,2,0:T(8,128)(2,1)S(1)} %copy.51), channel_id=1, source_target_pairs={{0,32},{32,0},{1,33},{33,1},{2,34},{34,2},{3,35},{35,3},{4,36},{36... | collective-permute-start | bytes 4915208 | tf_op jit(solution)/shard_map/ppermute | solution.py:15
  129.8 23.0 %collective-permute-start.2 = (f16[128,801]{0,1:T(8,128)(2,1)}, f16[128,801]{0,1:T(8,128)(2,1)}, u32[]{:S(2)}, u32[]{:S(2)}) collective-permute-start(f16[128,801]{0,1:T(8,128)(2,1)} %get-tuple-element.13), channel_id=1, source_target_pairs={{0,256},{256,0},{1,257},{257,1},{2,258},{258,2},{3,259},{259,3},{4... | collective-permute-start | bytes 615176 | tf_op jit(solution)/shard_map/ppermute | solution.py:15
  174.5 13.6 %collective-permute-start.3 = (f16[512,801]{0,1:T(8,128)(2,1)}, f16[512,801]{0,1:T(8,128)(2,1)}, u32[]{:S(2)}, u32[]{:S(2)}) collective-permute-start(f16[512,801]{0,1:T(8,128)(2,1)} %all_gather.10), channel_id=1, source_target_pairs={{0,32},{32,0},{1,33},{33,1},{2,34},{34,2},{3,35},{35,3},{4,36},{36... | collective-permute-start | bytes 2460680 | tf_op jit(solution)/shard_map/ppermute | solution.py:15
  177.4 22.6 %all-to-all-start.3 = ((bf16[16,64,320]{2,1,0:T(8,128)(2,1)}), bf16[16,64,320]{2,1,0:T(8,128)(2,1)}, u32[]{:S(2)}, u32[]{:S(2)}) async-start(bf16[16,64,320]{2,1,0:T(8,128)(2,1)} %broadcast_in_dim.20), calls=%async_computation.3 | async-start | bytes 1572864 | tf_op jit(solution)/shard_map/all_to_all | solution.py:50
  191.7 1.9 copy-start.1
  191.7 1.9 copy-start.3
  191.7 1.9 copy-start.5
  191.7 1.9 copy-start.7
  200.0 17.8 %all-to-all-start.2 = ((bf16[16,64,320]{2,1,0:T(8,128)(2,1)}), bf16[16,64,320]{2,1,0:T(8,128)(2,1)S(1)}, u32[]{:S(2)}, u32[]{:S(2)}) async-start(bf16[16,64,320]{2,1,0:T(8,128)(2,1)} %bitcast.18), calls=%async_computation.2 | async-start | bytes 1572864 | tf_op jit(solution)/shard_map/all_to_all | solution.py:102
  205.3 3.9 %copy-start.2 = (bf16[512,800]{0,1:T(8,128)(2,1)S(1)}, bf16[512,800]{0,1:T(8,128)(2,1)}, u32[]{:S(2)}) copy-start(bf16[512,800]{0,1:T(8,128)(2,1)} %copy-done.1) | copy-start | bytes 2457604
  205.3 3.9 %copy-start.4 = (bf16[512,800]{0,1:T(8,128)(2,1)S(1)}, bf16[512,800]{0,1:T(8,128)(2,1)}, u32[]{:S(2)}) copy-start(bf16[512,800]{0,1:T(8,128)(2,1)} %copy-done.3) | copy-start | bytes 2457604
  205.3 3.9 %copy-start.6 = (bf16[512,800]{0,1:T(8,128)(2,1)S(1)}, bf16[512,800]{0,1:T(8,128)(2,1)}, u32[]{:S(2)}) copy-start(bf16[512,800]{0,1:T(8,128)(2,1)} %copy-done.5) | copy-start | bytes 2457604
  205.3 3.9 %copy-start.8 = (bf16[512,800]{0,1:T(8,128)(2,1)S(1)}, bf16[512,800]{0,1:T(8,128)(2,1)}, u32[]{:S(2)}) copy-start(bf16[512,800]{0,1:T(8,128)(2,1)} %copy-done.7) | copy-start | bytes 2457604
  217.9 14.9 %collective-permute-start.5 = (f32[32,320]{1,0:T(8,128)S(1)}, f32[32,320]{1,0:T(8,128)S(1)}, u32[]{:S(2)}, u32[]{:S(2)}) collective-permute-start(f32[32,320]{1,0:T(8,128)S(1)} %constant_dynamic-slice_fusion), channel_id=1, source_target_pairs={{0,1},{1,0},{2,3},{3,2},{4,5},{5,4},{6,7},{7,6},{8,9},{9,8},{10,11... | collective-permute-start | bytes 122888 | tf_op jit(solution)/shard_map/ppermute | solution.py:15
  (3 other events, 4.5 us)
Sparse Core Ops, SparseCore 0:
  39.2 79.7 all-gather.1

commit v2 on v1

v2 whole, which is shorter than its diff:
```python
import jax
import jax.numpy as jnp
from jax import lax
from jax.sharding import Mesh
from jax.sharding import PartitionSpec as P

F32, F16, BF16 = jnp.float32, jnp.float16, jnp.bfloat16

SIZES = dict(p=2, q=2, r=2, c=2, y=4, v=2, w=2, h=2)
ROW, COL = ("p", "q", "r", "c"), ("y", "v", "w", "h")
LINE, QUAD, PLANE = ("p", "q", "r"), ("q", "r"), ("w", "y", "v")
UNITS = 200
TAIL = 8


def swap(x, axis):
    return lax.ppermute(x, axis, [(0, 1), (1, 0)])


def halves(x, at):
    n = x.shape[0] // 2
    return (
        lax.dynamic_slice_in_dim(x, at * n, n, 0),
        lax.dynamic_slice_in_dim(x, (1 - at) * n, n, 0),
    )


def dot(left, right, of_left, of_right):
    return lax.dot_general(
        left, right, (((of_left,), (of_right,)), ((), ())), preferred_element_type=F32
    )


def encode(x, power):
    tail = jnp.broadcast_to(power, x.shape[:-2] + (TAIL, x.shape[-1]))
    return jnp.concatenate([x * jnp.exp2(power), tail], axis=-2).astype(F16)


def decode(coded):
    wide = coded.astype(F32)
    power = wide[..., UNITS : UNITS + 1, :]
    return wide[..., :UNITS, :] * jnp.exp2(-power), power


def plane_gather(x):
    got = lax.all_to_all(jnp.broadcast_to(x[None], (16,) + x.shape), PLANE, 0, 0, tiled=True)
    return got.reshape((16 * x.shape[0],) + x.shape[1:])


def largest(*arrays):
    return jnp.max(jnp.stack([jnp.max(jnp.abs(a)) for a in arrays])).astype(F32)


def opening(grad_output, activations, down_weight):
    core, run = lax.axis_index("c"), lax.axis_index("h")
    near = jnp.stack([grad_output, activations])
    away = swap(near, "h")
    pair = jnp.concatenate(
        [jnp.where(run == 0, near, away), jnp.where(run == 0, away, near)], axis=1
    )
    grad_rows = plane_gather(pair[0])
    down_other = swap(down_weight, "c")

    mine, theirs = halves(grad_rows, core)
    given = swap(theirs, "c")
    part = dot(down_weight, mine, 1, 1) + dot(down_other, given, 1, 1)
    bound = 640.0 * largest(grad_rows, given) * largest(down_weight, down_other)
    power = jnp.clip(13.0 - jnp.ceil(jnp.log2(bound)), -100.0, 100.0)
    coded = encode(part.reshape(4, UNITS, 512), jnp.full((1, 1, 512), power))
    return coded, grad_rows, pair[1]


def shards(activations, grad_output, gate_pre, up_pre, gate_weight, up_weight, down_weight):
    core, run = lax.axis_index("c"), lax.axis_index("h")

    saved = lax.all_gather(jnp.stack([gate_pre, up_pre]), LINE, axis=1, tiled=True)
    coded, grad_rows, act_pair = lax.cond(
        run < 2,
        opening,
        lambda *_: (
            jnp.zeros((4, UNITS + TAIL, 512), F16),
            jnp.zeros((1024, 320), BF16),
            jnp.zeros((64, 320), BF16),
        ),
        grad_output,
        activations,
        down_weight,
    )

    saved_other = swap(saved, "c")
    parts, powers = decode(lax.all_to_all(coded, QUAD, 0, 0, tiled=True))
    coded = encode(jnp.sum(parts, axis=0), jnp.min(powers, axis=0) - 2.0)
    coded, act_pair = lax.optimization_barrier((coded, act_pair))
    far = swap(coded, "p")
    act_rows = plane_gather(act_pair)

    def by_core(own, other):
        first = jnp.where(core == 0, own, other)
        second = jnp.where(core == 0, other, own)
        return jnp.concatenate([first, second], axis=1)

    gate_wide = by_core(saved[0].T, saved_other[0].T).astype(F32)
    up_wide = by_core(saved[1].T, saved_other[1].T).astype(F32)
    logistic = jax.nn.sigmoid(gate_wide)
    silu_val = gate_wide * logistic
    hidden = (silu_val * up_wide).astype(BF16)
    gate_slope = up_wide * logistic * (1.0 + gate_wide * (1.0 - logistic))

    part, power = decode(coded)
    far_part, far_power = decode(far)
    coded = encode(part + far_part, jnp.minimum(power, far_power) - 1.0)
    coded, act_rows, silu_val, gate_slope, hidden = lax.optimization_barrier(
        (coded, act_rows, silu_val, gate_slope, hidden)
    )
    coded = lax.all_gather(coded, QUAD, axis=0, tiled=False)
    coded_other = swap(coded, "c")

    grad_down_weight = dot(hidden, grad_rows, 1, 0)

    own, other = decode(coded)[0].reshape(800, 512), decode(coded_other)[0].reshape(800, 512)
    grad_hidden = by_core(own, other)
    grad_gate = (grad_hidden * gate_slope).astype(BF16)
    grad_up = (grad_hidden * silu_val).astype(BF16)

    share = dot(grad_gate, gate_weight, 0, 1) + dot(grad_up, up_weight, 0, 1)
    share = lax.all_to_all(share.astype(BF16).reshape(16, 64, 320), PLANE, 0, 0, tiled=True)
    share = jnp.sum(share.astype(F32), axis=0)
    near, away = halves(share, run)
    grad_input = near + swap(away, "h")

    grad_gate_weight = dot(act_rows, grad_gate, 0, 1)
    grad_up_weight = dot(act_rows, grad_up, 0, 1)
    return (grad_input, grad_gate_weight, grad_up_weight, grad_down_weight)


def solution(mesh):
    fine = Mesh(mesh.devices.reshape(tuple(SIZES.values())), tuple(SIZES))
    wide, units, down = P(COL, ROW), P(ROW, COL), P(COL, ROW)
    return jax.shard_map(
        shards,
        mesh=fine,
        in_specs=(wide, wide, units, units, units, units, down),
        out_specs=(wide, units, units, down),
        check_vma=False,
    )
```

time: 242 us -> 210 us (0.87)
  waiting for transfers between devices: 96 us -> 32.3 us
  blocking collectives: 35.7 us -> 52.5 us
  starting transfers between devices: 45.2 us -> 59.7 us
  between operations: 18.8 us -> 14.3 us
  loops' own time: 0 us -> 2.81 us
  other arithmetic: 15 us -> 17.7 us
    all_gather x1, waiting for transfers between devices: 55.9 us -> 0.02 us  [shards(): lax.all_gather(jnp.stack([gate_pre, up_pre]), LINE, axis=1, tiled=True)]
    all_to_all x0 -> x1, blocking collectives: none -> 34 us  [shards(): parts, powers = decode(lax.all_to_all(coded, QUAD, 0, 0, tiled=True))]
    ppermute x6 -> x7, starting transfers between devices: 18.9 us -> 38.7 us  [swap(): return lax.ppermute(x, axis, [(0, 1), (1, 0)])]
    all_gather x2 -> x1, blocking collectives: 35.7 us -> 18.5 us  [shards(): coded = lax.all_gather(coded, QUAD, axis=0, tiled=False)]
    ppermute x6 -> x7, waiting for transfers between devices: 23.1 us -> 16.9 us  [swap(): return lax.ppermute(x, axis, [(0, 1), (1, 0)])]
    convert_element_type x0 -> x1, other arithmetic: none -> 4.04 us  [shards(): hidden = (silu_val * up_wide).astype(BF16)]
    convert_element_type x5, other arithmetic: 5.68 us -> 2.61 us  [decode(): wide = coded.astype(F32)]
    all_to_all x2 -> x1, starting transfers between devices: 9.49 us -> 6.49 us  [shards(): lax.all_to_all(share.astype(BF16).reshape(16, 64, 320), PLANE, 0, 0, tile...]
  transfers between devices with their start and end apart: 11 -> 11, of which waited for: 6 -> 6; matrix products, arithmetic and copies ran while one was open for 18% -> 15% of each run, Pallas kernels for 0% -> 0%
where the time goes in v2:
time: 210 us; the launch traced here: 209 us
  starting transfers between devices  59.7 us (28%)
  blocking collectives  52.5 us (25%)
  waiting for transfers between devices  32.3 us (15%)
  other arithmetic  17.7 us (8%)
  matrix products  15.4 us (7%)
  between operations  14.3 us (7%)
  local copies, waits for them, and re-layouts  14.1 us (7%)
  loops' own time  2.81 us (1%)
    ppermute x7, starting transfers between devices, swap(): return lax.ppermute(x, axis, [(0, 1), (1, 0)])  38.7 us
    all_to_all x1, blocking collectives, shards(): parts, powers = decode(lax.all_to_all(coded, QUAD, 0, 0, tiled=True))  34 us
    all_gather x1, blocking collectives, shards(): coded = lax.all_gather(coded, QUAD, axis=0, tiled=False)  18.5 us
    ppermute x7, waiting for transfers between devices, swap(): return lax.ppermute(x, axis, [(0, 1), (1, 0)])  16.9 us
    dot_general x7, matrix products, dot(): lax.dot_general(left, right, (((of_left,), (of_right,)), ((), ())), prefe...  15.4 us
    all_to_all x2, starting transfers between devices, plane_gather(): lax.all_to_all(jnp.broadcast_to(x[None], (16,) + x.shape), PLANE, 0, 0, t...  14.5 us
    all_to_all x2, waiting for transfers between devices, plane_gather(): lax.all_to_all(jnp.broadcast_to(x[None], (16,) + x.shape), PLANE, 0, 0, t...  9.11 us
    all_to_all x1, starting transfers between devices, shards(): lax.all_to_all(share.astype(BF16).reshape(16, 64, 320), PLANE, 0, 0, tile...  6.49 us
  transfers between devices with their start and end apart: 11, of which 6 were waited for; matrix products, arithmetic and copies ran while one was open for 15% of the time, Pallas kernels for 0%

profile of v2, /device:TPU:4, one launch (start us, length us, event | category | flops | bytes accessed | tf_op | source)
XLA Modules:
  0.0 208.9 jit_solution(8651746320384432465)
XLA Ops:
  9.2 50.2 %conditional.1 = (f16[4,208,512]{2,1,0:T(8,128)(2,1)}, bf16[1024,320]{1,0:T(8,128)(2,1)S(1)}, bf16[64,320]{1,0:T(8,128)(2,1)S(1)}) conditional(s32[]{:T(128)} %convert_element_type.48, () %tuple.18, (bf16[32,320]{1,0:T(8,128)(2,1)}, bf16[32,320]{1,0:T(8,128)(2,1)}, bf16[800,320]{0,1:T(8,128)(2,1)}) %tuple.19), branch_computations={%region_0.0_spmd, %region_1.6_spmd} | conditional | flops 527769600 | bytes 26370646 | solution.py:77
  10.1 15.7 %collective-permute-start = (bf16[2,32,320]{2,1,0:T(8,128)(2,1)S(1)}, bf16[2,32,320]{2,1,0:T(8,128)(2,1)S(1)}, u32[]{:S(2)}, u32[]{:S(2)}) collective-permute-start(bf16[2,32,320]{2,1,0:T(8,128)(2,1)S(1)} %pad_maximum_fusion.1), channel_id=1, source_target_pairs={{0,1},{1,0},{2,3},{3,2},{4,5},{5,4},{6,7},{7,6},{8,9},{9,8},{10,11... | collective-permute-start | bytes 122888 | tf_op jit(solution)/shard_map/cond/branch_1_fun/ppermute | solution.py:17
  25.8 1.9 collective-permute-start.2
  30.5 7.4 %all-to-all-start = ((bf16[16,64,320]{2,1,0:T(8,128)(2,1)}), bf16[16,64,320]{2,1,0:T(8,128)(2,1)S(1)}, u32[]{:S(2)}, u32[]{:S(2)}) async-start(bf16[16,64,320]{2,1,0:T(8,128)(2,1)} %broadcast_in_dim.12), calls=%async_computation | async-start | bytes 1572864 | tf_op jit(solution)/shard_map/cond/branch_1_fun/all_to_all | solution.py:46
  40.7 9.1 %all-to-all-done = bf16[16,64,320]{2,1,0:T(8,128)(2,1)S(1)} async-done(((bf16[16,64,320]{2,1,0:T(8,128)(2,1)}), bf16[16,64,320]{2,1,0:T(8,128)(2,1)S(1)}, u32[]{:S(2)}, u32[]{:S(2)}) %all-to-all-start) | async-done | bytes 655392 | tf_op jit(solution)/shard_map/cond/branch_1_fun/all_to_all | solution.py:46
  49.9 1.9 collective-permute-start.1
  56.5 1.7 multiply_convert_fusion
  59.4 34.0 %all_to_all.19 = f16[4,208,512]{2,1,0:T(8,128)(2,1)S(1)} all-to-all(f16[4,208,512]{2,1,0:T(8,128)(2,1)} %get-tuple-element.23), channel_id=1, replica_groups=mesh['p'=2,'q'=2,'r'=2,'c'=2,'y'=4,'v'=2,'w'=2,'h'=2] {'q','r'}, dimensions={0} | all-to-all | bytes 1703936 | tf_op jit(solution)/shard_map/all_to_all | solution.py:91
  93.7 5.4 %copy.35 = bf16[2,512,800]{1,2,0:T(8,128)(2,1)} copy(bf16[2,512,800]{2,0,1:T(2,128)(2,1)} %all-gather.3.cloned.1.call-done) | data formatting | bytes 3276800 | tf_op jit(solution)/shard_map/all_gather | solution.py:76
  99.2 2.0 collective-permute-start.4
  102.2 6.1 %collective-permute-start.3 = (f16[208,512]{1,0:T(8,128)(2,1)}, f16[208,512]{1,0:T(8,128)(2,1)}, u32[]{:S(2)}, u32[]{:S(2)}) collective-permute-start(f16[208,512]{1,0:T(8,128)(2,1)} %pad_maximum_fusion.6), channel_id=1, source_target_pairs={{0,256},{256,0},{1,257},{257,1},{2,258},{258,2},{3,259},{259,3},{4... | collective-permute-start | bytes 638984 | tf_op jit(solution)/shard_map/ppermute | solution.py:17
  110.2 7.0 %all-to-all-start.2 = ((bf16[16,64,320]{2,1,0:T(8,128)(2,1)}), bf16[16,64,320]{2,1,0:T(8,128)(2,1)}, u32[]{:S(2)}, u32[]{:S(2)}) async-start(bf16[16,64,320]{2,1,0:T(8,128)(2,1)} %broadcast_in_dim.30), calls=%async_computation.2 | async-start | bytes 1572864 | tf_op jit(solution)/shard_map/all_to_all | solution.py:46
  117.3 12.0 %collective-permute-done.3 = f16[208,512]{1,0:T(8,128)(2,1)} collective-permute-done((f16[208,512]{1,0:T(8,128)(2,1)}, f16[208,512]{1,0:T(8,128)(2,1)}, u32[]{:S(2)}, u32[]{:S(2)}) %collective-permute-start.3) | collective-permute-done | bytes 213024 | tf_op jit(solution)/shard_map/ppermute | solution.py:17
  132.1 4.0 %fusion.7 = (bf16[800,1024]{1,0:T(8,128)(2,1)}, f32[800,1024]{1,0:T(8,128)}, f32[800,1024]{1,0:T(8,128)}) fusion(bf16[800,512]{1,0:T(8,128)(2,1)S(1)} %get-tuple-element.59, bf16[800,512]{1,0:T(8,128)(2,1)S(1)} %get-tuple-element.57, bf16[800,512]{1,0:T(8,128)(2,1)S(1)} %get-tuple-element.58, bf16[800,512]{1,0:T(8,128)(2,1)S(1)} %get-tuple-element.60), kind=kLoop, calls=%fused_computation.24 | loop fusion | flops 15564800 | bytes 11468800 | tf_op jit(solution)/shard_map/convert_element_type | solution.py:106
  136.1 18.5 %all-gather = f16[832,512]{1,0:T(8,128)(2,1)S(1)} all-gather(f16[208,512]{1,0:T(8,128)(2,1)S(1)} %pad_maximum_fusion.7), channel_id=2, replica_groups=mesh['p'=2,'q'=2,'r'=2,'c'=2,'y'=4,'v'=2,'w'=2,'h'=2] {'q','r'}, dimensions={0}, use_global_device_ids=true | all-gather | bytes 1064960 | tf_op jit(solution)/shard_map/all_gather | solution.py:115
  154.6 1.9 collective-permute-start.5
  156.8 2.1 collective-permute-done.5
  167.2 6.5 %all-to-all-start.3 = ((bf16[16,64,320]{2,1,0:T(8,128)(2,1)}), bf16[16,64,320]{2,1,0:T(8,128)(2,1)S(1)}, u32[]{:S(2)}, u32[]{:S(2)}) async-start(bf16[16,64,320]{2,1,0:T(8,128)(2,1)} %bitcast.24), calls=%async_computation.3 | async-start | bytes 1572864 | tf_op jit(solution)/shard_map/all_to_all | solution.py:126
  173.7 3.4 %fusion.25 = f32[800,320]{0,1:T(8,128)} fusion(bf16[800,1024]{1,0:T(8,128)(2,1)} %get-tuple-element.31, bf16[1024,320]{1,0:T(8,128)(2,1)S(1)} %get-tuple-element.32), kind=kOutput, calls=%fused_computation.78 | convolution fusion | flops 524288000 | bytes 3317760 | tf_op jit(solution)/shard_map/dot_general | solution.py:29
  177.1 3.2 %fusion.23 = f32[320,800]{1,0:T(8,128)} fusion(bf16[1024,320]{1,0:T(8,128)(2,1)} %bitcast.10, bf16[800,1024]{1,0:T(8,128)(2,1)S(1)} %copy-done.10), kind=kOutput, calls=%fused_computation.76 | convolution fusion | flops 524288000 | bytes 3317760 | tf_op jit(solution)/shard_map/dot_general | solution.py:29
  180.3 6.3 %all-to-all-done.3 = bf16[16,64,320]{2,1,0:T(8,128)(2,1)S(1)} async-done(((bf16[16,64,320]{2,1,0:T(8,128)(2,1)}), bf16[16,64,320]{2,1,0:T(8,128)(2,1)S(1)}, u32[]{:S(2)}, u32[]{:S(2)}) %all-to-all-start.3) | async-done | bytes 655392 | tf_op jit(solution)/shard_map/all_to_all | solution.py:126
  186.8 9.2 %collective-permute-start.6 = (f32[32,320]{1,0:T(8,128)S(1)}, f32[32,320]{1,0:T(8,128)S(1)}, u32[]{:S(2)}, u32[]{:S(2)}) collective-permute-start(f32[32,320]{1,0:T(8,128)S(1)} %constant_dynamic-slice_fusion.1), channel_id=1, source_target_pairs={{0,1},{1,0},{2,3},{3,2},{4,5},{5,4},{6,7},{7,6},{8,9},{9,8},{10,11... | collective-permute-start | bytes 122888 | tf_op jit(solution)/shard_map/ppermute | solution.py:17
  195.9 3.7 %fusion.24 = f32[320,800]{1,0:T(8,128)} fusion(bf16[1024,320]{1,0:T(8,128)(2,1)} %bitcast.10, bf16[800,1024]{1,0:T(8,128)(2,1)} %copy-done.8), kind=kOutput, calls=%fused_computation.77 | convolution fusion | flops 524288000 | bytes 3317760 | tf_op jit(solution)/shard_map/dot_general | solution.py:29
  199.6 1.8 collective-permute-done.6
  (76 shorter events, 26.8 us)
Async XLA Ops:
  7.2 156.3 %copy-start = (bf16[320,800]{1,0:T(8,128)(2,1)S(1)}, bf16[320,800]{1,0:T(8,128)(2,1)}, u32[]{:S(2)}) copy-start(bf16[320,800]{1,0:T(8,128)(2,1)} %param.14) | copy-start | bytes 1536004
  7.2 86.5 %all-gather.3.cloned.1.call-start = ((), (), s32[]{:S(2)}) async-start(), calls=%async_computation.4 | async-start | bytes 2064384 | tf_op jit(solution)/shard_map/all_gather | solution.py:76
  9.2 28.7 %copy-start.7 = (bf16[800,320]{0,1:T(8,128)(2,1)S(1)}, bf16[800,320]{0,1:T(8,128)(2,1)}, u32[]{:S(2)}) copy-start(bf16[800,320]{0,1:T(8,128)(2,1)} %get-tuple-element.38) | copy-start | bytes 1536004 | tf_op jit(solution)/shard_map/cond
  10.1 18.7 %collective-permute-start = (bf16[2,32,320]{2,1,0:T(8,128)(2,1)S(1)}, bf16[2,32,320]{2,1,0:T(8,128)(2,1)S(1)}, u32[]{:S(2)}, u32[]{:S(2)}) collective-permute-start(bf16[2,32,320]{2,1,0:T(8,128)(2,1)S(1)} %pad_maximum_fusion.1), channel_id=1, source_target_pairs={{0,1},{1,0},{2,3},{3,2},{4,5},{5,4},{6,7},{7,6},{8,9},{9,8},{10,11... | collective-permute-start | bytes 122888 | tf_op jit(solution)/shard_map/cond/branch_1_fun/ppermute | solution.py:17
  25.8 12.9 %collective-permute-start.2 = (bf16[800,320]{0,1:T(8,128)(2,1)}, bf16[800,320]{0,1:T(8,128)(2,1)S(1)}, u32[]{:S(2)}, u32[]{:S(2)}) collective-permute-start(bf16[800,320]{0,1:T(8,128)(2,1)} %get-tuple-element.38), channel_id=1, source_target_pairs={{0,32},{32,0},{1,33},{33,1},{2,34},{34,2},{3,35},{35,3},{4,36},{36... | collective-permute-start | bytes 1536008 | tf_op jit(solution)/shard_map/cond/branch_1_fun/ppermute | solution.py:17
  30.5 19.3 %all-to-all-start = ((bf16[16,64,320]{2,1,0:T(8,128)(2,1)}), bf16[16,64,320]{2,1,0:T(8,128)(2,1)S(1)}, u32[]{:S(2)}, u32[]{:S(2)}) async-start(bf16[16,64,320]{2,1,0:T(8,128)(2,1)} %broadcast_in_dim.12), calls=%async_computation | async-start | bytes 1572864 | tf_op jit(solution)/shard_map/cond/branch_1_fun/all_to_all | solution.py:46
  38.7 13.1 %copy-start.6 = (bf16[800,320]{0,1:T(8,128)(2,1)}, bf16[800,320]{0,1:T(8,128)(2,1)S(1)}, u32[]{:S(2)}) copy-start(bf16[800,320]{0,1:T(8,128)(2,1)S(1)} %collective-permute-done.2) | copy-start | bytes 1536004 | tf_op jit(solution)/shard_map/cond
  49.8 4.5 %copy-start.3 = (bf16[16,64,320]{2,1,0:T(8,128)(2,1)}, bf16[16,64,320]{2,1,0:T(8,128)(2,1)S(1)}, u32[]{:S(2)}) copy-start(bf16[16,64,320]{2,1,0:T(8,128)(2,1)S(1)} %all-to-all-done) | copy-start | bytes 1966084 | tf_op jit(solution)/shard_map/cond
  49.9 4.5 %collective-permute-start.1 = (bf16[512,320]{1,0:T(8,128)(2,1)S(1)}, bf16[512,320]{1,0:T(8,128)(2,1)S(1)}, u32[]{:S(2)}, u32[]{:S(2)}) collective-permute-start(bf16[512,320]{1,0:T(8,128)(2,1)S(1)} %constant_dynamic-slice_fusion), channel_id=1, source_target_pairs={{0,32},{32,0},{1,33},{33,1},{2,34},{34,2},{3,35},{35,3},{4,36},{36... | collective-permute-start | bytes 983048 | tf_op jit(solution)/shard_map/cond/branch_1_fun/ppermute | solution.py:17
  58.2 1.2 copy-start.4
  99.2 31.3 %collective-permute-start.4 = (bf16[2,512,800]{1,2,0:T(8,128)(2,1)}, bf16[2,512,800]{1,2,0:T(8,128)(2,1)}, u32[]{:S(2)}, u32[]{:S(2)}) collective-permute-start(bf16[2,512,800]{1,2,0:T(8,128)(2,1)} %copy.35), channel_id=1, source_target_pairs={{0,32},{32,0},{1,33},{33,1},{2,34},{34,2},{3,35},{35,3},{4,36},{36... | collective-permute-start | bytes 4915208 | tf_op jit(solution)/shard_map/ppermute | solution.py:17
  102.2 27.1 %collective-permute-start.3 = (f16[208,512]{1,0:T(8,128)(2,1)}, f16[208,512]{1,0:T(8,128)(2,1)}, u32[]{:S(2)}, u32[]{:S(2)}) collective-permute-start(f16[208,512]{1,0:T(8,128)(2,1)} %pad_maximum_fusion.6), channel_id=1, source_target_pairs={{0,256},{256,0},{1,257},{257,1},{2,258},{258,2},{3,259},{259,3},{4... | collective-permute-start | bytes 638984 | tf_op jit(solution)/shard_map/ppermute | solution.py:17
  110.2 20.2 %copy-start.5 = (bf16[2,512,800]{1,2,0:T(8,128)(2,1)S(1)}, bf16[2,512,800]{1,2,0:T(8,128)(2,1)}, u32[]{:S(2)}) copy-start(bf16[2,512,800]{1,2,0:T(8,128)(2,1)} %copy.35) | copy-start | bytes 4915204
  110.2 25.9 %all-to-all-start.2 = ((bf16[16,64,320]{2,1,0:T(8,128)(2,1)}), bf16[16,64,320]{2,1,0:T(8,128)(2,1)}, u32[]{:S(2)}, u32[]{:S(2)}) async-start(bf16[16,64,320]{2,1,0:T(8,128)(2,1)} %broadcast_in_dim.30), calls=%async_computation.2 | async-start | bytes 1572864 | tf_op jit(solution)/shard_map/all_to_all | solution.py:46
  154.6 4.3 %collective-permute-start.5 = (f16[4,208,512]{2,1,0:T(8,128)(2,1)S(1)}, f16[4,208,512]{2,1,0:T(8,128)(2,1)S(1)}, u32[]{:S(2)}, u32[]{:S(2)}) collective-permute-start(f16[4,208,512]{2,1,0:T(8,128)(2,1)S(1)} %bitcast.63), channel_id=1, source_target_pairs={{0,32},{32,0},{1,33},{33,1},{2,34},{34,2},{3,35},{35,3},{4,36},{36... | collective-permute-start | bytes 2555912 | tf_op jit(solution)/shard_map/ppermute | solution.py:17
  159.2 1.9 copy-start.1
  159.2 2.9 %copy-start.2 = (f32[800,1024]{1,0:T(8,128)S(1)}, f32[800,1024]{1,0:T(8,128)}, u32[]{:S(2)}) copy-start(f32[800,1024]{1,0:T(8,128)} %get-tuple-element.29) | copy-start | bytes 9830404
  163.5 1.2 copy-start.8
  163.5 1.7 copy-start.9
  163.5 1.7 copy-start.11
  167.2 19.4 %all-to-all-start.3 = ((bf16[16,64,320]{2,1,0:T(8,128)(2,1)}), bf16[16,64,320]{2,1,0:T(8,128)(2,1)S(1)}, u32[]{:S(2)}, u32[]{:S(2)}) async-start(bf16[16,64,320]{2,1,0:T(8,128)(2,1)} %bitcast.24), calls=%async_computation.3 | async-start | bytes 1572864 | tf_op jit(solution)/shard_map/all_to_all | solution.py:126
  173.7 3.5 %copy-start.10 = (bf16[800,1024]{1,0:T(8,128)(2,1)S(1)}, bf16[800,1024]{1,0:T(8,128)(2,1)}, u32[]{:S(2)}) copy-start(bf16[800,1024]{1,0:T(8,128)(2,1)} %copy-done.9) | copy-start | bytes 4915204
  186.8 14.7 %collective-permute-start.6 = (f32[32,320]{1,0:T(8,128)S(1)}, f32[32,320]{1,0:T(8,128)S(1)}, u32[]{:S(2)}, u32[]{:S(2)}) collective-permute-start(f32[32,320]{1,0:T(8,128)S(1)} %constant_dynamic-slice_fusion.1), channel_id=1, source_target_pairs={{0,1},{1,0},{2,3},{3,2},{4,5},{5,4},{6,7},{7,6},{8,9},{9,8},{10,11... | collective-permute-start | bytes 122888 | tf_op jit(solution)/shard_map/ppermute | solution.py:17
Sparse Core Ops, SparseCore 0:
  10.1 77.6 all-gather.2

commit v3 on v2

--- a/solution.py
+++ b/solution.py
@@ -1,6 +1,7 @@
 import jax
 import jax.numpy as jnp
 from jax import lax
+from jax.experimental.layout import Layout, with_layout_constraint
 from jax.sharding import Mesh
 from jax.sharding import PartitionSpec as P
 
@@ -73,7 +74,8 @@
 def shards(activations, grad_output, gate_pre, up_pre, gate_weight, up_weight, down_weight):
     core, run = lax.axis_index("c"), lax.axis_index("h")
 
-    saved = lax.all_gather(jnp.stack([gate_pre, up_pre]), LINE, axis=1, tiled=True)
+    saved = jnp.pad(jnp.concatenate([gate_pre, up_pre]), ((0, 0), (0, 96)))
+    saved = lax.all_gather(saved, LINE, axis=0, tiled=False)
     coded, grad_rows, act_pair = lax.cond(
         run < 2,
         opening,
@@ -99,19 +101,25 @@
         second = jnp.where(core == 0, other, own)
         return jnp.concatenate([first, second], axis=1)
 
-    gate_wide = by_core(saved[0].T, saved_other[0].T).astype(F32)
-    up_wide = by_core(saved[1].T, saved_other[1].T).astype(F32)
+    def turned(rows):
+        rows = rows[..., :800].reshape(512, 800).T
+        return with_layout_constraint(rows, Layout(major_to_minor=(0, 1)))
+
+    def projection(rows):
+        return by_core(turned(saved[:, rows]), turned(saved_other[:, rows])).astype(F32)
+
+    gate_wide, up_wide = projection(slice(0, 64)), projection(slice(64, 128))
     logistic = jax.nn.sigmoid(gate_wide)
     silu_val = gate_wide * logistic
     hidden = (silu_val * up_wide).astype(BF16)
     gate_slope = up_wide * logistic * (1.0 + gate_wide * (1.0 - logistic))
 
+    far, act_rows, silu_val, gate_slope, hidden = lax.optimization_barrier(
+        (far, act_rows, silu_val, gate_slope, hidden)
+    )
     part, power = decode(coded)
     far_part, far_power = decode(far)
     coded = encode(part + far_part, jnp.minimum(power, far_power) - 1.0)
-    coded, act_rows, silu_val, gate_slope, hidden = lax.optimization_barrier(
-        (coded, act_rows, silu_val, gate_slope, hidden)
-    )
     coded = lax.all_gather(coded, QUAD, axis=0, tiled=False)
     coded_other = swap(coded, "c")
 
@@ -123,7 +131,8 @@
     grad_up = (grad_hidden * silu_val).astype(BF16)
 
     share = dot(grad_gate, gate_weight, 0, 1) + dot(grad_up, up_weight, 0, 1)
-    share = lax.all_to_all(share.astype(BF16).reshape(16, 64, 320), PLANE, 0, 0, tiled=True)
+    share = with_layout_constraint(share.astype(BF16), Layout(major_to_minor=(0, 1)))
+    share = lax.all_to_all(share.reshape(16, 64, 320), PLANE, 0, 0, tiled=True)
     share = jnp.sum(share.astype(F32), axis=0)
     near, away = halves(share, run)
     grad_input = near + swap(away, "h")

time: 210 us -> 201 us (0.957)
  blocking collectives: 52.5 us -> 19.6 us
  waiting for transfers between devices: 32.3 us -> 50.5 us
  starting transfers between devices: 59.7 us -> 63.2 us
    all_to_all x1 -> x0, blocking collectives: 34 us -> none  [shards(): parts, powers = decode(lax.all_to_all(coded, QUAD, 0, 0, tiled=True))]
    all_gather x1, waiting for transfers between devices: 0.02 us -> 26.2 us  [shards(): saved = lax.all_gather(saved, LINE, axis=0, tiled=False)]
    ppermute x7, waiting for transfers between devices: 16.9 us -> 5.87 us  [swap(): return lax.ppermute(x, axis, [(0, 1), (1, 0)])]
    all_gather x1 -> x0, local copies, waits for them, and re-layouts: 5.44 us -> none  [shards(): lax.all_gather(jnp.stack([gate_pre, up_pre]), LINE, axis=1, tiled=True)]
    reshape x0 -> x4, local copies, waits for them, and re-layouts: none -> 4.91 us  [turned(): rows = rows[..., :800].reshape(512, 800).T]
    all_to_all x1 -> x2, starting transfers between devices: 6.49 us -> 10.7 us  [the longest x1 7.22 us: shards(): share = lax.all_to_all(share.reshape(16, 64, 320), PLANE, 0, 0, tiled=True)]
    slice x0 -> x2, local copies, waits for them, and re-layouts: none -> 3.21 us  [turned(): rows = rows[..., :800].reshape(512, 800).T]
    all_to_all x1 -> x2, waiting for transfers between devices: 6.32 us -> 9.15 us  [the longest x1 6.31 us: shards(): share = lax.all_to_all(share.reshape(16, 64, 320), PLANE, 0, 0, tiled=True)]
  transfers between devices with their start and end apart: 11 -> 12, of which waited for: 6 -> 7; matrix products, arithmetic and copies ran while one was open for 15% -> 19% of each run, Pallas kernels for 0% -> 0%
where the time goes in v3:
time: 201 us; the launch traced here: 199 us
  starting transfers between devices  63.2 us (31%)
  waiting for transfers between devices  50.5 us (25%)
  blocking collectives  19.6 us (10%)
  other arithmetic  17.7 us (9%)
  matrix products  17.2 us (9%)
  between operations  14.4 us (7%)
  local copies, waits for them, and re-layouts  14.3 us (7%)
  loops' own time  2.65 us (1%)
    ppermute x7, starting transfers between devices, swap(): return lax.ppermute(x, axis, [(0, 1), (1, 0)])  38.1 us
    all_gather x1, waiting for transfers between devices, shards(): saved = lax.all_gather(saved, LINE, axis=0, tiled=False)  26.2 us
    all_gather x1, blocking collectives, shards(): coded = lax.all_gather(coded, QUAD, axis=0, tiled=False)  19.6 us
    dot_general x7, matrix products, dot(): lax.dot_general(left, right, (((of_left,), (of_right,)), ((), ())), prefe...  17.2 us
    all_to_all x2, starting transfers between devices, plane_gather(): lax.all_to_all(jnp.broadcast_to(x[None], (16,) + x.shape), PLANE, 0, 0, t...  14.3 us
    all_to_all x2, waiting for transfers between devices, plane_gather(): lax.all_to_all(jnp.broadcast_to(x[None], (16,) + x.shape), PLANE, 0, 0, t...  9.2 us
    all_to_all x1, starting transfers between devices, shards(): share = lax.all_to_all(share.reshape(16, 64, 320), PLANE, 0, 0, tiled=True)  7.22 us
    all_to_all x1, waiting for transfers between devices, shards(): share = lax.all_to_all(share.reshape(16, 64, 320), PLANE, 0, 0, tiled=True)  6.31 us
  transfers between devices with their start and end apart: 12, of which 7 were waited for; matrix products, arithmetic and copies ran while one was open for 19% of the time, Pallas kernels for 0%

profile of v3, /device:TPU:4, one launch (start us, length us, event | category | flops | bytes accessed | tf_op | source)
XLA Modules:
  0.0 199.4 jit_solution(2515451890161016579)
XLA Ops:
  9.0 50.1 %conditional.1 = (f16[4,208,512]{2,1,0:T(8,128)(2,1)}, bf16[1024,320]{1,0:T(8,128)(2,1)S(1)}, bf16[64,320]{1,0:T(8,128)(2,1)S(1)}) conditional(s32[]{:T(128)} %convert_element_type.57, () %tuple.18, (bf16[32,320]{1,0:T(8,128)(2,1)}, bf16[32,320]{1,0:T(8,128)(2,1)}, bf16[800,320]{0,1:T(8,128)(2,1)}) %tuple.19), branch_computations={%region_0.1_spmd, %region_1.6_spmd} | conditional | flops 527769600 | bytes 26370646 | solution.py:79
  9.8 15.7 %collective-permute-start = (bf16[2,32,320]{2,1,0:T(8,128)(2,1)S(1)}, bf16[2,32,320]{2,1,0:T(8,128)(2,1)S(1)}, u32[]{:S(2)}, u32[]{:S(2)}) collective-permute-start(bf16[2,32,320]{2,1,0:T(8,128)(2,1)S(1)} %pad_maximum_fusion.1), channel_id=1, source_target_pairs={{0,1},{1,0},{2,3},{3,2},{4,5},{5,4},{6,7},{7,6},{8,9},{9,8},{10,11... | collective-permute-start | bytes 122888 | tf_op jit(solution)/shard_map/cond/branch_1_fun/ppermute | solution.py:18
  25.6 1.9 collective-permute-start.2
  30.3 7.4 %all-to-all-start = ((bf16[16,64,320]{2,1,0:T(8,128)(2,1)}), bf16[16,64,320]{2,1,0:T(8,128)(2,1)S(1)}, u32[]{:S(2)}, u32[]{:S(2)}) async-start(bf16[16,64,320]{2,1,0:T(8,128)(2,1)} %broadcast_in_dim.11), calls=%async_computation | async-start | bytes 1572864 | tf_op jit(solution)/shard_map/cond/branch_1_fun/all_to_all | solution.py:47
  40.4 9.2 %all-to-all-done = bf16[16,64,320]{2,1,0:T(8,128)(2,1)S(1)} async-done(((bf16[16,64,320]{2,1,0:T(8,128)(2,1)}), bf16[16,64,320]{2,1,0:T(8,128)(2,1)S(1)}, u32[]{:S(2)}, u32[]{:S(2)}) %all-to-all-start) | async-done | bytes 655392 | tf_op jit(solution)/shard_map/cond/branch_1_fun/all_to_all | solution.py:47
  49.6 1.9 collective-permute-start.1
  59.0 3.5 %all-to-all-start.1 = ((f16[4,208,512]{2,1,0:T(8,128)(2,1)}), f16[4,208,512]{2,1,0:T(8,128)(2,1)S(1)}, u32[]{:S(2)}, u32[]{:S(2)}) async-start(f16[4,208,512]{2,1,0:T(8,128)(2,1)} %get-tuple-element.23), calls=%async_computation.1 | async-start | bytes 1703936 | tf_op jit(solution)/shard_map/all_to_all | solution.py:93
  62.5 26.2 %all-gather.3.cloned.1.call-done = bf16[1024,896]{1,0:T(8,128)(2,1)} async-done(((bf16[128,896]{1,0:T(8,128)(2,1)}), bf16[1024,896]{1,0:T(8,128)(2,1)}) %all-gather.3.cloned.1.call-update) | async-done | bytes 1835024 | tf_op jit(solution)/shard_map/all_gather | solution.py:78
  88.8 1.9 collective-permute-start.4
  90.7 2.8 %all-to-all-done.1 = f16[4,208,512]{2,1,0:T(8,128)(2,1)S(1)} async-done(((f16[4,208,512]{2,1,0:T(8,128)(2,1)}), f16[4,208,512]{2,1,0:T(8,128)(2,1)S(1)}, u32[]{:S(2)}, u32[]{:S(2)}) %all-to-all-start.1) | async-done | bytes 852000 | tf_op jit(solution)/shard_map/all_to_all | solution.py:93
  94.2 6.0 %collective-permute-start.3 = (f16[208,512]{1,0:T(8,128)(2,1)S(1)}, f16[208,512]{1,0:T(8,128)(2,1)}, u32[]{:S(2)}, u32[]{:S(2)}) collective-permute-start(f16[208,512]{1,0:T(8,128)(2,1)S(1)} %pad_maximum_fusion.5), channel_id=1, source_target_pairs={{0,256},{256,0},{1,257},{257,1},{2,258},{258,2},{3,259},{259,3},{4... | collective-permute-start | bytes 638984 | tf_op jit(solution)/shard_map/ppermute | solution.py:18
  102.0 6.9 %all-to-all-start.2 = ((bf16[16,64,320]{2,1,0:T(8,128)(2,1)}), bf16[16,64,320]{2,1,0:T(8,128)(2,1)}, u32[]{:S(2)}, u32[]{:S(2)}) async-start(bf16[16,64,320]{2,1,0:T(8,128)(2,1)} %broadcast_in_dim.16), calls=%async_computation.2 | async-start | bytes 1572864 | tf_op jit(solution)/shard_map/all_to_all | solution.py:47
  118.9 4.0 %fusion.7 = (bf16[800,1024]{1,0:T(8,128)(2,1)}, f32[800,1024]{1,0:T(8,128)}, f32[800,1024]{1,0:T(8,128)}) fusion(bf16[800,512]{1,0:T(8,128)(2,1)S(1)} %get-tuple-element.65, bf16[800,512]{1,0:T(8,128)(2,1)S(1)} %get-tuple-element.64, bf16[800,512]{1,0:T(8,128)(2,1)S(1)} %get-tuple-element.72, bf16[800,512]{1,0:T(8,128)(2,1)S(1)} %get-tuple-element.73), kind=kLoop, calls=%fused_computation.24 | loop fusion | flops 15564800 | bytes 11468800 | tf_op jit(solution)/shard_map/convert_element_type | solution.py:114
  124.1 19.6 %all_gather.12 = f16[4,208,512]{2,1,0:T(8,128)(2,1)S(1)} all-gather(f16[1,208,512]{2,1,0:T(8,128)(2,1)S(1)} %pad_maximum_fusion.6), channel_id=1, replica_groups=mesh['p'=2,'q'=2,'r'=2,'c'=2,'y'=4,'v'=2,'w'=2,'h'=2] {'q','r'}, dimensions={0}, use_global_device_ids=true | all-gather | bytes 1064960 | tf_op jit(solution)/shard_map/all_gather | solution.py:123
  143.7 1.9 collective-permute-start.5
  145.9 2.1 %collective-permute-done.5 = f16[4,208,512]{2,1,0:T(8,128)(2,1)S(1)} collective-permute-done((f16[4,208,512]{2,1,0:T(8,128)(2,1)S(1)}, f16[4,208,512]{2,1,0:T(8,128)(2,1)S(1)}, u32[]{:S(2)}, u32[]{:S(2)}) %collective-permute-start.5) | collective-permute-done | bytes 852000 | tf_op jit(solution)/shard_map/ppermute | solution.py:18
  154.2 2.1 %add_convert_fusion = bf16[1024,320]{1,0:T(8,128)(2,1)} fusion(f32[1024,320]{1,0:T(8,128)S(1)} %fusion.28, bf16[800,1024]{1,0:T(8,128)(2,1)S(1)} %get-tuple-element.53, bf16[320,800]{1,0:T(8,128)(2,1)S(1)} %copy-done.12), kind=kOutput, calls=%fused_computation.39 | convolution fusion | flops 524943360 | bytes 4116480 | tf_op jit(solution)/shard_map/dot_general | solution.py:30
  156.4 7.2 %all-to-all-start.3 = ((bf16[16,64,320]{2,1,0:T(8,128)(2,1)}), bf16[16,64,320]{2,1,0:T(8,128)(2,1)S(1)}, u32[]{:S(2)}, u32[]{:S(2)}) async-start(bf16[16,64,320]{2,1,0:T(8,128)(2,1)} %bitcast.23), calls=%async_computation.3 | async-start | bytes 1572864 | tf_op jit(solution)/shard_map/all_to_all | solution.py:135
  163.6 3.4 %fusion.31 = f32[800,320]{0,1:T(8,128)} fusion(bf16[800,1024]{1,0:T(8,128)(2,1)} %get-tuple-element.31, bf16[1024,320]{1,0:T(8,128)(2,1)S(1)} %get-tuple-element.32), kind=kOutput, calls=%fused_computation.84 | convolution fusion | flops 524288000 | bytes 3317760 | tf_op jit(solution)/shard_map/dot_general | solution.py:30
  167.1 3.2 %fusion.29 = f32[320,800]{1,0:T(8,128)} fusion(bf16[1024,320]{1,0:T(8,128)(2,1)} %bitcast.8, bf16[800,1024]{1,0:T(8,128)(2,1)S(1)} %copy-done.11), kind=kOutput, calls=%fused_computation.82 | convolution fusion | flops 524288000 | bytes 3317760 | tf_op jit(solution)/shard_map/dot_general | solution.py:30
  170.3 6.3 %all-to-all-done.3 = bf16[16,64,320]{2,1,0:T(8,128)(2,1)S(1)} async-done(((bf16[16,64,320]{2,1,0:T(8,128)(2,1)}), bf16[16,64,320]{2,1,0:T(8,128)(2,1)S(1)}, u32[]{:S(2)}, u32[]{:S(2)}) %all-to-all-start.3) | async-done | bytes 655392 | tf_op jit(solution)/shard_map/all_to_all | solution.py:135
  176.7 8.7 %collective-permute-start.6 = (f32[32,320]{1,0:T(8,128)S(1)}, f32[32,320]{1,0:T(8,128)S(1)}, u32[]{:S(2)}, u32[]{:S(2)}) collective-permute-start(f32[32,320]{1,0:T(8,128)S(1)} %constant_dynamic-slice_fusion.1), channel_id=1, source_target_pairs={{0,1},{1,0},{2,3},{3,2},{4,5},{5,4},{6,7},{7,6},{8,9},{9,8},{10,11... | collective-permute-start | bytes 122888 | tf_op jit(solution)/shard_map/ppermute | solution.py:18
  185.4 3.7 %fusion.30 = f32[320,800]{1,0:T(8,128)} fusion(bf16[1024,320]{1,0:T(8,128)(2,1)} %bitcast.8, bf16[800,1024]{1,0:T(8,128)(2,1)} %copy-done.9), kind=kOutput, calls=%fused_computation.83 | convolution fusion | flops 524288000 | bytes 3317760 | tf_op jit(solution)/shard_map/dot_general | solution.py:30
  189.1 2.8 %collective-permute-done.6 = f32[32,320]{1,0:T(8,128)S(1)} collective-permute-done((f32[32,320]{1,0:T(8,128)S(1)}, f32[32,320]{1,0:T(8,128)S(1)}, u32[]{:S(2)}, u32[]{:S(2)}) %collective-permute-start.6) | collective-permute-done | bytes 40992 | tf_op jit(solution)/shard_map/ppermute | solution.py:18
  (82 shorter events, 33.7 us)
Async XLA Ops:
  7.2 145.4 %copy-start = (bf16[320,800]{1,0:T(8,128)(2,1)S(1)}, bf16[320,800]{1,0:T(8,128)(2,1)}, u32[]{:S(2)}) copy-start(bf16[320,800]{1,0:T(8,128)(2,1)} %param.14) | copy-start | bytes 1536004
  7.2 81.6 %all-gather.3.cloned.1.call-start = ((), (), s32[]{:S(2)}) async-start(), calls=%async_computation.4 | async-start | bytes 2064384 | tf_op jit(solution)/shard_map/all_gather | solution.py:78
  9.0 28.7 %copy-start.7 = (bf16[800,320]{0,1:T(8,128)(2,1)S(1)}, bf16[800,320]{0,1:T(8,128)(2,1)}, u32[]{:S(2)}) copy-start(bf16[800,320]{0,1:T(8,128)(2,1)} %get-tuple-element.38) | copy-start | bytes 1536004 | tf_op jit(solution)/shard_map/cond
  9.8 18.7 %collective-permute-start = (bf16[2,32,320]{2,1,0:T(8,128)(2,1)S(1)}, bf16[2,32,320]{2,1,0:T(8,128)(2,1)S(1)}, u32[]{:S(2)}, u32[]{:S(2)}) collective-permute-start(bf16[2,32,320]{2,1,0:T(8,128)(2,1)S(1)} %pad_maximum_fusion.1), channel_id=1, source_target_pairs={{0,1},{1,0},{2,3},{3,2},{4,5},{5,4},{6,7},{7,6},{8,9},{9,8},{10,11... | collective-permute-start | bytes 122888 | tf_op jit(solution)/shard_map/cond/branch_1_fun/ppermute | solution.py:18
  25.6 12.9 %collective-permute-start.2 = (bf16[800,320]{0,1:T(8,128)(2,1)}, bf16[800,320]{0,1:T(8,128)(2,1)S(1)}, u32[]{:S(2)}, u32[]{:S(2)}) collective-permute-start(bf16[800,320]{0,1:T(8,128)(2,1)} %get-tuple-element.38), channel_id=1, source_target_pairs={{0,32},{32,0},{1,33},{33,1},{2,34},{34,2},{3,35},{35,3},{4,36},{36... | collective-permute-start | bytes 1536008 | tf_op jit(solution)/shard_map/cond/branch_1_fun/ppermute | solution.py:18
  30.3 19.3 %all-to-all-start = ((bf16[16,64,320]{2,1,0:T(8,128)(2,1)}), bf16[16,64,320]{2,1,0:T(8,128)(2,1)S(1)}, u32[]{:S(2)}, u32[]{:S(2)}) async-start(bf16[16,64,320]{2,1,0:T(8,128)(2,1)} %broadcast_in_dim.11), calls=%async_computation | async-start | bytes 1572864 | tf_op jit(solution)/shard_map/cond/branch_1_fun/all_to_all | solution.py:47
  38.4 13.1 %copy-start.6 = (bf16[800,320]{0,1:T(8,128)(2,1)}, bf16[800,320]{0,1:T(8,128)(2,1)S(1)}, u32[]{:S(2)}) copy-start(bf16[800,320]{0,1:T(8,128)(2,1)S(1)} %collective-permute-done.2) | copy-start | bytes 1536004 | tf_op jit(solution)/shard_map/cond
  49.6 4.5 %copy-start.3 = (bf16[16,64,320]{2,1,0:T(8,128)(2,1)}, bf16[16,64,320]{2,1,0:T(8,128)(2,1)S(1)}, u32[]{:S(2)}) copy-start(bf16[16,64,320]{2,1,0:T(8,128)(2,1)S(1)} %all-to-all-done) | copy-start | bytes 1966084 | tf_op jit(solution)/shard_map/cond
  49.6 4.5 %collective-permute-start.1 = (bf16[512,320]{1,0:T(8,128)(2,1)S(1)}, bf16[512,320]{1,0:T(8,128)(2,1)S(1)}, u32[]{:S(2)}, u32[]{:S(2)}) collective-permute-start(bf16[512,320]{1,0:T(8,128)(2,1)S(1)} %constant_dynamic-slice_fusion), channel_id=1, source_target_pairs={{0,32},{32,0},{1,33},{33,1},{2,34},{34,2},{3,35},{35,3},{4,36},{36... | collective-permute-start | bytes 983048 | tf_op jit(solution)/shard_map/cond/branch_1_fun/ppermute | solution.py:18
  59.0 34.5 %all-to-all-start.1 = ((f16[4,208,512]{2,1,0:T(8,128)(2,1)}), f16[4,208,512]{2,1,0:T(8,128)(2,1)S(1)}, u32[]{:S(2)}, u32[]{:S(2)}) async-start(f16[4,208,512]{2,1,0:T(8,128)(2,1)} %get-tuple-element.23), calls=%async_computation.1 | async-start | bytes 1703936 | tf_op jit(solution)/shard_map/all_to_all | solution.py:93
  88.8 24.1 %collective-permute-start.4 = (bf16[8,128,896]{2,1,0:T(8,128)(2,1)}, bf16[8,128,896]{2,1,0:T(8,128)(2,1)}, u32[]{:S(2)}, u32[]{:S(2)}) collective-permute-start(bf16[8,128,896]{2,1,0:T(8,128)(2,1)} %bitcast.68), channel_id=1, source_target_pairs={{0,32},{32,0},{1,33},{33,1},{2,34},{34,2},{3,35},{35,3},{4,36},{36... | collective-permute-start | bytes 5505032 | tf_op jit(solution)/shard_map/ppermute | solution.py:18
  94.2 28.7 %collective-permute-start.3 = (f16[208,512]{1,0:T(8,128)(2,1)S(1)}, f16[208,512]{1,0:T(8,128)(2,1)}, u32[]{:S(2)}, u32[]{:S(2)}) collective-permute-start(f16[208,512]{1,0:T(8,128)(2,1)S(1)} %pad_maximum_fusion.5), channel_id=1, source_target_pairs={{0,256},{256,0},{1,257},{257,1},{2,258},{258,2},{3,259},{259,3},{4... | collective-permute-start | bytes 638984 | tf_op jit(solution)/shard_map/ppermute | solution.py:18
  102.0 20.9 %all-to-all-start.2 = ((bf16[16,64,320]{2,1,0:T(8,128)(2,1)}), bf16[16,64,320]{2,1,0:T(8,128)(2,1)}, u32[]{:S(2)}, u32[]{:S(2)}) async-start(bf16[16,64,320]{2,1,0:T(8,128)(2,1)} %broadcast_in_dim.16), calls=%async_computation.2 | async-start | bytes 1572864 | tf_op jit(solution)/shard_map/all_to_all | solution.py:47
  115.8 1.3 copy-start.5
  118.9 5.0 %copy-start.8 = (f32[208,512]{1,0:T(8,128)S(1)}, f32[208,512]{1,0:T(8,128)}, u32[]{:S(2)}) copy-start(f32[208,512]{1,0:T(8,128)} %convert_element_type.59) | copy-start | bytes 1277956
  143.7 4.3 %collective-permute-start.5 = (f16[4,208,512]{2,1,0:T(8,128)(2,1)S(1)}, f16[4,208,512]{2,1,0:T(8,128)(2,1)S(1)}, u32[]{:S(2)}, u32[]{:S(2)}) collective-permute-start(f16[4,208,512]{2,1,0:T(8,128)(2,1)S(1)} %all_gather.12), channel_id=1, source_target_pairs={{0,32},{32,0},{1,33},{33,1},{2,34},{34,2},{3,35},{35,3},{4,36},{36... | collective-permute-start | bytes 2555912 | tf_op jit(solution)/shard_map/ppermute | solution.py:18
  148.2 1.9 copy-start.1
  148.3 2.9 %copy-start.2 = (f32[800,1024]{1,0:T(8,128)S(1)}, f32[800,1024]{1,0:T(8,128)}, u32[]{:S(2)}) copy-start(f32[800,1024]{1,0:T(8,128)} %get-tuple-element.29) | copy-start | bytes 9830404
  152.6 1.3 copy-start.9
  152.6 1.7 copy-start.10
  152.6 1.6 copy-start.12
  156.4 20.2 %all-to-all-start.3 = ((bf16[16,64,320]{2,1,0:T(8,128)(2,1)}), bf16[16,64,320]{2,1,0:T(8,128)(2,1)S(1)}, u32[]{:S(2)}, u32[]{:S(2)}) async-start(bf16[16,64,320]{2,1,0:T(8,128)(2,1)} %bitcast.23), calls=%async_computation.3 | async-start | bytes 1572864 | tf_op jit(solution)/shard_map/all_to_all | solution.py:135
  163.6 3.5 %copy-start.11 = (bf16[800,1024]{1,0:T(8,128)(2,1)S(1)}, bf16[800,1024]{1,0:T(8,128)(2,1)}, u32[]{:S(2)}) copy-start(bf16[800,1024]{1,0:T(8,128)(2,1)} %copy-done.10) | copy-start | bytes 4915204
  176.7 15.2 %collective-permute-start.6 = (f32[32,320]{1,0:T(8,128)S(1)}, f32[32,320]{1,0:T(8,128)S(1)}, u32[]{:S(2)}, u32[]{:S(2)}) collective-permute-start(f32[32,320]{1,0:T(8,128)S(1)} %constant_dynamic-slice_fusion.1), channel_id=1, source_target_pairs={{0,1},{1,0},{2,3},{3,2},{4,5},{5,4},{6,7},{7,6},{8,9},{9,8},{10,11... | collective-permute-start | bytes 122888 | tf_op jit(solution)/shard_map/ppermute | solution.py:18
  (1 other events, 1.2 us)
Sparse Core Ops, SparseCore 0:
  10.1 78.6 all-gather.2

commit v4 on v3

--- a/solution.py
+++ b/solution.py
@@ -53,13 +53,12 @@
 
 
 def opening(grad_output, activations, down_weight):
-    core, run = lax.axis_index("c"), lax.axis_index("h")
+    core = lax.axis_index("c")
     near = jnp.stack([grad_output, activations])
-    away = swap(near, "h")
-    pair = jnp.concatenate(
-        [jnp.where(run == 0, near, away), jnp.where(run == 0, away, near)], axis=1
-    )
+    pair = jnp.concatenate([near, swap(near, "h")], axis=1)
     grad_rows = plane_gather(pair[0])
+    down_weight = jnp.pad(down_weight.reshape(4, UNITS, 320), ((0, 0), (0, TAIL), (0, 0)))
+    down_weight = down_weight.reshape(4 * (UNITS + TAIL), 320)
     down_other = swap(down_weight, "c")
 
     mine, theirs = halves(grad_rows, core)
@@ -67,14 +66,18 @@
     part = dot(down_weight, mine, 1, 1) + dot(down_other, given, 1, 1)
     bound = 640.0 * largest(grad_rows, given) * largest(down_weight, down_other)
     power = jnp.clip(13.0 - jnp.ceil(jnp.log2(bound)), -100.0, 100.0)
-    coded = encode(part.reshape(4, UNITS, 512), jnp.full((1, 1, 512), power))
+    part = part.reshape(4, UNITS + TAIL, 512)
+    tail = lax.broadcasted_iota(jnp.int32, part.shape, 1) >= UNITS
+    coded = jnp.where(tail, power, part * jnp.exp2(power)).astype(F16)
     return coded, grad_rows, pair[1]
 
 
 def shards(activations, grad_output, gate_pre, up_pre, gate_weight, up_weight, down_weight):
     core, run = lax.axis_index("c"), lax.axis_index("h")
 
-    saved = jnp.pad(jnp.concatenate([gate_pre, up_pre]), ((0, 0), (0, 96)))
+    saved = jnp.stack([gate_pre, up_pre]).reshape(2, 2, 32, 800)
+    saved = jnp.where(run == 0, saved, saved[:, ::-1]).reshape(128, 800)
+    saved = jnp.pad(saved, ((0, 0), (0, 96)))
     saved = lax.all_gather(saved, LINE, axis=0, tiled=False)
     coded, grad_rows, act_pair = lax.cond(
         run < 2,
@@ -134,8 +137,7 @@
     share = with_layout_constraint(share.astype(BF16), Layout(major_to_minor=(0, 1)))
     share = lax.all_to_all(share.reshape(16, 64, 320), PLANE, 0, 0, tiled=True)
     share = jnp.sum(share.astype(F32), axis=0)
-    near, away = halves(share, run)
-    grad_input = near + swap(away, "h")
+    grad_input = share[:32] + swap(share[32:], "h")
 
     grad_gate_weight = dot(act_rows, grad_gate, 0, 1)
     grad_up_weight = dot(act_rows, grad_up, 0, 1)

time: 201 us -> 200 us (level)
  no operation moved by 1% of the time
where the time goes in v4:
time: 200 us; the launch traced here: 199 us
  starting transfers between devices  63 us (32%)
  waiting for transfers between devices  50.4 us (25%)
  blocking collectives  19.1 us (10%)
  other arithmetic  17.5 us (9%)
  matrix products  16.1 us (8%)
  local copies, waits for them, and re-layouts  15.5 us (8%)
  between operations  14.4 us (7%)
  loops' own time  2.84 us (1%)
    ppermute x7, starting transfers between devices, swap(): return lax.ppermute(x, axis, [(0, 1), (1, 0)])  38.3 us
    all_gather x1, waiting for transfers between devices, shards(): saved = lax.all_gather(saved, LINE, axis=0, tiled=False)  25.5 us
    all_gather x1, blocking collectives, shards(): coded = lax.all_gather(coded, QUAD, axis=0, tiled=False)  19.1 us
    dot_general x7, matrix products, dot(): lax.dot_general(left, right, (((of_left,), (of_right,)), ((), ())), prefe...  16.1 us
    all_to_all x2, starting transfers between devices, plane_gather(): lax.all_to_all(jnp.broadcast_to(x[None], (16,) + x.shape), PLANE, 0, 0, t...  13.9 us
    all_to_all x2, waiting for transfers between devices, plane_gather(): lax.all_to_all(jnp.broadcast_to(x[None], (16,) + x.shape), PLANE, 0, 0, t...  11.1 us
    all_to_all x1, starting transfers between devices, shards(): share = lax.all_to_all(share.reshape(16, 64, 320), PLANE, 0, 0, tiled=True)  7.22 us
    all_to_all x1, waiting for transfers between devices, shards(): share = lax.all_to_all(share.reshape(16, 64, 320), PLANE, 0, 0, tiled=True)  6.32 us
  transfers between devices with their start and end apart: 12, of which 7 were waited for; matrix products, arithmetic and copies ran while one was open for 19% of the time, Pallas kernels for 0%

profile of v4, /device:TPU:4, one launch (start us, length us, event | category | flops | bytes accessed | tf_op | source)
XLA Modules:
  0.0 198.8 jit_solution(9097080631052196061)
XLA Ops:
  9.1 51.5 %conditional.1 = (f16[4,208,512]{2,1,0:T(8,128)(2,1)}, bf16[1024,320]{1,0:T(8,128)(2,1)S(1)}, bf16[64,320]{1,0:T(8,128)(2,1)S(1)}) conditional(s32[]{:T(128)} %convert_element_type.61, () %tuple.18, (bf16[32,320]{1,0:T(8,128)(2,1)}, bf16[32,320]{1,0:T(8,128)(2,1)}, bf16[800,320]{0,1:T(8,128)(2,1)}) %tuple.19), branch_computations={%region_0.1_spmd, %region_1.6_spmd} | conditional | flops 549810368 | bytes 33600552 | solution.py:82
  9.8 15.7 %collective-permute-start = (bf16[2,32,320]{2,1,0:T(8,128)(2,1)S(1)}, bf16[2,32,320]{2,1,0:T(8,128)(2,1)S(1)}, u32[]{:S(2)}, u32[]{:S(2)}) collective-permute-start(bf16[2,32,320]{2,1,0:T(8,128)(2,1)S(1)} %pad_maximum_fusion.1), channel_id=1, source_target_pairs={{0,1},{1,0},{2,3},{3,2},{4,5},{5,4},{6,7},{7,6},{8,9},{9,8},{10,11... | collective-permute-start | bytes 122888 | tf_op jit(solution)/shard_map/cond/branch_1_fun/ppermute | solution.py:18
  28.1 1.9 collective-permute-start.2
  31.1 7.4 %all-to-all-start = ((bf16[16,64,320]{2,1,0:T(8,128)(2,1)}), bf16[16,64,320]{2,1,0:T(8,128)(2,1)S(1)}, u32[]{:S(2)}, u32[]{:S(2)}) async-start(bf16[16,64,320]{2,1,0:T(8,128)(2,1)} %broadcast_in_dim.12), calls=%async_computation | async-start | bytes 1572864 | tf_op jit(solution)/shard_map/cond/branch_1_fun/all_to_all | solution.py:47
  40.6 11.1 %all-to-all-done = bf16[16,64,320]{2,1,0:T(8,128)(2,1)S(1)} async-done(((bf16[16,64,320]{2,1,0:T(8,128)(2,1)}), bf16[16,64,320]{2,1,0:T(8,128)(2,1)S(1)}, u32[]{:S(2)}, u32[]{:S(2)}) %all-to-all-start) | async-done | bytes 655392 | tf_op jit(solution)/shard_map/cond/branch_1_fun/all_to_all | solution.py:47
  51.8 2.1 %collective-permute-start.1 = (bf16[512,320]{1,0:T(8,128)(2,1)S(1)}, bf16[512,320]{1,0:T(8,128)(2,1)S(1)}, u32[]{:S(2)}, u32[]{:S(2)}) collective-permute-start(bf16[512,320]{1,0:T(8,128)(2,1)S(1)} %constant_dynamic-slice_fusion), channel_id=1, source_target_pairs={{0,32},{32,0},{1,33},{33,1},{2,34},{34,2},{3,35},{35,3},{4,36},{36... | collective-permute-start | bytes 983048 | tf_op jit(solution)/shard_map/cond/branch_1_fun/ppermute | solution.py:18
  60.5 3.5 %all-to-all-start.1 = ((f16[4,208,512]{2,1,0:T(8,128)(2,1)}), f16[4,208,512]{2,1,0:T(8,128)(2,1)S(1)}, u32[]{:S(2)}, u32[]{:S(2)}) async-start(f16[4,208,512]{2,1,0:T(8,128)(2,1)} %get-tuple-element.23), calls=%async_computation.1 | async-start | bytes 1703936 | tf_op jit(solution)/shard_map/all_to_all | solution.py:96
  64.0 25.5 %all-gather.3.cloned.1.call-done = bf16[1024,896]{1,0:T(8,128)(2,1)} async-done(((bf16[128,896]{1,0:T(8,128)(2,1)}), bf16[1024,896]{1,0:T(8,128)(2,1)}) %all-gather.3.cloned.1.call-update) | async-done | bytes 1835024 | tf_op jit(solution)/shard_map/all_gather | solution.py:81
  89.5 1.9 collective-permute-start.4
  91.4 2.5 %all-to-all-done.1 = f16[4,208,512]{2,1,0:T(8,128)(2,1)S(1)} async-done(((f16[4,208,512]{2,1,0:T(8,128)(2,1)}), f16[4,208,512]{2,1,0:T(8,128)(2,1)S(1)}, u32[]{:S(2)}, u32[]{:S(2)}) %all-to-all-start.1) | async-done | bytes 852000 | tf_op jit(solution)/shard_map/all_to_all | solution.py:96
  94.6 5.4 %collective-permute-start.3 = (f16[208,512]{1,0:T(8,128)(2,1)S(1)}, f16[208,512]{1,0:T(8,128)(2,1)}, u32[]{:S(2)}, u32[]{:S(2)}) collective-permute-start(f16[208,512]{1,0:T(8,128)(2,1)S(1)} %pad_maximum_fusion.6), channel_id=1, source_target_pairs={{0,256},{256,0},{1,257},{257,1},{2,258},{258,2},{3,259},{259,3},{4... | collective-permute-start | bytes 638984 | tf_op jit(solution)/shard_map/ppermute | solution.py:18
  101.8 6.4 %all-to-all-start.2 = ((bf16[16,64,320]{2,1,0:T(8,128)(2,1)}), bf16[16,64,320]{2,1,0:T(8,128)(2,1)}, u32[]{:S(2)}, u32[]{:S(2)}) async-start(bf16[16,64,320]{2,1,0:T(8,128)(2,1)} %broadcast_in_dim.28), calls=%async_computation.2 | async-start | bytes 1572864 | tf_op jit(solution)/shard_map/all_to_all | solution.py:47
  118.2 4.0 %fusion.4 = (bf16[800,1024]{1,0:T(8,128)(2,1)}, f32[800,1024]{1,0:T(8,128)}, f32[800,1024]{1,0:T(8,128)}) fusion(bf16[800,512]{1,0:T(8,128)(2,1)S(1)} %get-tuple-element.68, bf16[800,512]{1,0:T(8,128)(2,1)S(1)} %get-tuple-element.67, bf16[800,512]{1,0:T(8,128)(2,1)S(1)} %get-tuple-element.75, bf16[800,512]{1,0:T(8,128)(2,1)S(1)} %get-tuple-element.76), kind=kLoop, calls=%fused_computation.21 | loop fusion | flops 15564800 | bytes 11468800 | tf_op jit(solution)/shard_map/convert_element_type | solution.py:117
  123.5 19.1 %all_gather.12 = f16[4,208,512]{2,1,0:T(8,128)(2,1)S(1)} all-gather(f16[1,208,512]{2,1,0:T(8,128)(2,1)S(1)} %pad_maximum_fusion.7), channel_id=1, replica_groups=mesh['p'=2,'q'=2,'r'=2,'c'=2,'y'=4,'v'=2,'w'=2,'h'=2] {'q','r'}, dimensions={0}, use_global_device_ids=true | all-gather | bytes 1064960 | tf_op jit(solution)/shard_map/all_gather | solution.py:126
  142.5 2.1 %collective-permute-start.5 = (f16[4,208,512]{2,1,0:T(8,128)(2,1)S(1)}, f16[4,208,512]{2,1,0:T(8,128)(2,1)S(1)}, u32[]{:S(2)}, u32[]{:S(2)}) collective-permute-start(f16[4,208,512]{2,1,0:T(8,128)(2,1)S(1)} %all_gather.12), channel_id=1, source_target_pairs={{0,32},{32,0},{1,33},{33,1},{2,34},{34,2},{3,35},{35,3},{4,36},{36... | collective-permute-start | bytes 2555912 | tf_op jit(solution)/shard_map/ppermute | solution.py:18
  144.9 1.9 collective-permute-done.5
  153.1 2.1 %add_convert_fusion = bf16[1024,320]{1,0:T(8,128)(2,1)} fusion(f32[1024,320]{1,0:T(8,128)S(1)} %fusion.22, bf16[800,1024]{1,0:T(8,128)(2,1)S(1)} %get-tuple-element.56, bf16[320,800]{1,0:T(8,128)(2,1)S(1)} %copy-done.15), kind=kOutput, calls=%fused_computation.36 | convolution fusion | flops 524943360 | bytes 4116480 | tf_op jit(solution)/shard_map/dot_general | solution.py:30
  155.2 7.2 %all-to-all-start.3 = ((bf16[16,64,320]{2,1,0:T(8,128)(2,1)}), bf16[16,64,320]{2,1,0:T(8,128)(2,1)S(1)}, u32[]{:S(2)}, u32[]{:S(2)}) async-start(bf16[16,64,320]{2,1,0:T(8,128)(2,1)} %bitcast.27), calls=%async_computation.3 | async-start | bytes 1572864 | tf_op jit(solution)/shard_map/all_to_all | solution.py:138
  162.5 3.4 %fusion.25 = f32[800,320]{0,1:T(8,128)} fusion(bf16[800,1024]{1,0:T(8,128)(2,1)} %get-tuple-element.31, bf16[1024,320]{1,0:T(8,128)(2,1)S(1)} %get-tuple-element.32), kind=kOutput, calls=%fused_computation.78 | convolution fusion | flops 524288000 | bytes 3317760 | tf_op jit(solution)/shard_map/dot_general | solution.py:30
  165.9 3.2 %fusion.23 = f32[320,800]{1,0:T(8,128)} fusion(bf16[1024,320]{1,0:T(8,128)(2,1)} %bitcast.9, bf16[800,1024]{1,0:T(8,128)(2,1)S(1)} %copy-done.12), kind=kOutput, calls=%fused_computation.76 | convolution fusion | flops 524288000 | bytes 3317760 | tf_op jit(solution)/shard_map/dot_general | solution.py:30
  169.1 6.3 %all-to-all-done.3 = bf16[16,64,320]{2,1,0:T(8,128)(2,1)S(1)} async-done(((bf16[16,64,320]{2,1,0:T(8,128)(2,1)}), bf16[16,64,320]{2,1,0:T(8,128)(2,1)S(1)}, u32[]{:S(2)}, u32[]{:S(2)}) %all-to-all-start.3) | async-done | bytes 655392 | tf_op jit(solution)/shard_map/all_to_all | solution.py:138
  175.5 9.2 %collective-permute-start.6 = (f32[32,320]{1,0:T(8,128)S(1)}, f32[32,320]{1,0:T(8,128)S(1)}, u32[]{:S(2)}, u32[]{:S(2)}) collective-permute-start(f32[32,320]{1,0:T(8,128)S(1)} %slice.95), channel_id=1, source_target_pairs={{0,1},{1,0},{2,3},{3,2},{4,5},{5,4},{6,7},{7,6},{8,9},{9,8},{10,11... | collective-permute-start | bytes 122888 | tf_op jit(solution)/shard_map/ppermute | solution.py:18
  184.8 3.7 %fusion.24 = f32[320,800]{1,0:T(8,128)} fusion(bf16[1024,320]{1,0:T(8,128)(2,1)} %bitcast.9, bf16[800,1024]{1,0:T(8,128)(2,1)} %copy-done.10), kind=kOutput, calls=%fused_computation.77 | convolution fusion | flops 524288000 | bytes 3317760 | tf_op jit(solution)/shard_map/dot_general | solution.py:30
  188.5 2.8 %collective-permute-done.6 = f32[32,320]{1,0:T(8,128)S(1)} collective-permute-done((f32[32,320]{1,0:T(8,128)S(1)}, f32[32,320]{1,0:T(8,128)S(1)}, u32[]{:S(2)}, u32[]{:S(2)}) %collective-permute-start.6) | collective-permute-done | bytes 40992 | tf_op jit(solution)/shard_map/ppermute | solution.py:18
  (93 shorter events, 32.9 us)
Async XLA Ops:
  7.2 144.2 %copy-start = (bf16[320,800]{1,0:T(8,128)(2,1)S(1)}, bf16[320,800]{1,0:T(8,128)(2,1)}, u32[]{:S(2)}) copy-start(bf16[320,800]{1,0:T(8,128)(2,1)} %param.14) | copy-start | bytes 1536004
  7.2 82.3 %all-gather.3.cloned.1.call-start = ((), (), s32[]{:S(2)}) async-start(), calls=%async_computation.4 | async-start | bytes 2064384 | tf_op jit(solution)/shard_map/all_gather | solution.py:81
  9.8 20.2 %collective-permute-start = (bf16[2,32,320]{2,1,0:T(8,128)(2,1)S(1)}, bf16[2,32,320]{2,1,0:T(8,128)(2,1)S(1)}, u32[]{:S(2)}, u32[]{:S(2)}) collective-permute-start(bf16[2,32,320]{2,1,0:T(8,128)(2,1)S(1)} %pad_maximum_fusion.1), channel_id=1, source_target_pairs={{0,1},{1,0},{2,3},{3,2},{4,5},{5,4},{6,7},{7,6},{8,9},{9,8},{10,11... | collective-permute-start | bytes 122888 | tf_op jit(solution)/shard_map/cond/branch_1_fun/ppermute | solution.py:18
  25.6 4.5 %copy-start.13 = (bf16[32,320]{1,0:T(8,128)(2,1)S(1)}, bf16[32,320]{1,0:T(8,128)(2,1)}, u32[]{:S(2)}) copy-start(bf16[32,320]{1,0:T(8,128)(2,1)} %get-tuple-element.36) | copy-start | bytes 61444 | tf_op jit(solution)/shard_map/cond
  25.6 4.5 %copy-start.14 = (bf16[32,320]{1,0:T(8,128)(2,1)S(1)}, bf16[32,320]{1,0:T(8,128)(2,1)}, u32[]{:S(2)}) copy-start(bf16[32,320]{1,0:T(8,128)(2,1)} %get-tuple-element.37) | copy-start | bytes 61444 | tf_op jit(solution)/shard_map/cond
  27.8 3.3 %copy-start.5 = (bf16[4,208,320]{2,1,0:T(8,128)(2,1)}, bf16[4,208,320]{2,1,0:T(8,128)(2,1)S(1)}, u32[]{:S(2)}) copy-start(bf16[4,208,320]{2,1,0:T(8,128)(2,1)S(1)} %get-tuple-element.51) | copy-start | bytes 1597444 | tf_op jit(solution)/shard_map/cond
  28.1 10.4 %collective-permute-start.2 = (bf16[832,320]{0,1:T(8,128)(2,1)S(1)}, bf16[832,320]{0,1:T(8,128)(2,1)S(1)}, u32[]{:S(2)}, u32[]{:S(2)}) collective-permute-start(bf16[832,320]{0,1:T(8,128)(2,1)S(1)} %copy.25), channel_id=1, source_target_pairs={{0,32},{32,0},{1,33},{33,1},{2,34},{34,2},{3,35},{35,3},{4,36},{36... | collective-permute-start | bytes 1597448 | tf_op jit(solution)/shard_map/cond/branch_1_fun/ppermute | solution.py:18
  31.1 20.6 %all-to-all-start = ((bf16[16,64,320]{2,1,0:T(8,128)(2,1)}), bf16[16,64,320]{2,1,0:T(8,128)(2,1)S(1)}, u32[]{:S(2)}, u32[]{:S(2)}) async-start(bf16[16,64,320]{2,1,0:T(8,128)(2,1)} %broadcast_in_dim.12), calls=%async_computation | async-start | bytes 1572864 | tf_op jit(solution)/shard_map/cond/branch_1_fun/all_to_all | solution.py:47
  38.6 15.3 %copy-start.8 = (bf16[832,320]{0,1:T(8,128)(2,1)}, bf16[832,320]{0,1:T(8,128)(2,1)S(1)}, u32[]{:S(2)}) copy-start(bf16[832,320]{0,1:T(8,128)(2,1)S(1)} %collective-permute-done.2) | copy-start | bytes 1597444 | tf_op jit(solution)/shard_map/cond
  51.7 3.6 %copy-start.3 = (bf16[16,64,320]{2,1,0:T(8,128)(2,1)}, bf16[16,64,320]{2,1,0:T(8,128)(2,1)S(1)}, u32[]{:S(2)}) copy-start(bf16[16,64,320]{2,1,0:T(8,128)(2,1)S(1)} %all-to-all-done) | copy-start | bytes 1966084 | tf_op jit(solution)/shard_map/cond
  51.8 2.9 %copy-start.6 = (bf16[4,208,320]{2,1,0:T(8,128)(2,1)S(1)}, bf16[4,208,320]{2,1,0:T(8,128)(2,1)}, u32[]{:S(2)}) copy-start(bf16[4,208,320]{2,1,0:T(8,128)(2,1)} %copy-done.5) | copy-start | bytes 1597444 | tf_op jit(solution)/shard_map/cond
  51.8 3.7 %collective-permute-start.1 = (bf16[512,320]{1,0:T(8,128)(2,1)S(1)}, bf16[512,320]{1,0:T(8,128)(2,1)S(1)}, u32[]{:S(2)}, u32[]{:S(2)}) collective-permute-start(bf16[512,320]{1,0:T(8,128)(2,1)S(1)} %constant_dynamic-slice_fusion), channel_id=1, source_target_pairs={{0,32},{32,0},{1,33},{33,1},{2,34},{34,2},{3,35},{35,3},{4,36},{36... | collective-permute-start | bytes 983048 | tf_op jit(solution)/shard_map/cond/branch_1_fun/ppermute | solution.py:18
  60.5 33.4 %all-to-all-start.1 = ((f16[4,208,512]{2,1,0:T(8,128)(2,1)}), f16[4,208,512]{2,1,0:T(8,128)(2,1)S(1)}, u32[]{:S(2)}, u32[]{:S(2)}) async-start(f16[4,208,512]{2,1,0:T(8,128)(2,1)} %get-tuple-element.23), calls=%async_computation.1 | async-start | bytes 1703936 | tf_op jit(solution)/shard_map/all_to_all | solution.py:96
  89.5 22.7 %collective-permute-start.4 = (bf16[8,128,896]{2,1,0:T(8,128)(2,1)}, bf16[8,128,896]{2,1,0:T(8,128)(2,1)}, u32[]{:S(2)}, u32[]{:S(2)}) collective-permute-start(bf16[8,128,896]{2,1,0:T(8,128)(2,1)} %bitcast.74), channel_id=1, source_target_pairs={{0,32},{32,0},{1,33},{33,1},{2,34},{34,2},{3,35},{35,3},{4,36},{36... | collective-permute-start | bytes 5505032 | tf_op jit(solution)/shard_map/ppermute | solution.py:18
  94.6 27.7 %collective-permute-start.3 = (f16[208,512]{1,0:T(8,128)(2,1)S(1)}, f16[208,512]{1,0:T(8,128)(2,1)}, u32[]{:S(2)}, u32[]{:S(2)}) collective-permute-start(f16[208,512]{1,0:T(8,128)(2,1)S(1)} %pad_maximum_fusion.6), channel_id=1, source_target_pairs={{0,256},{256,0},{1,257},{257,1},{2,258},{258,2},{3,259},{259,3},{4... | collective-permute-start | bytes 638984 | tf_op jit(solution)/shard_map/ppermute | solution.py:18
  101.8 20.5 %all-to-all-start.2 = ((bf16[16,64,320]{2,1,0:T(8,128)(2,1)}), bf16[16,64,320]{2,1,0:T(8,128)(2,1)}, u32[]{:S(2)}, u32[]{:S(2)}) async-start(bf16[16,64,320]{2,1,0:T(8,128)(2,1)} %broadcast_in_dim.28), calls=%async_computation.2 | async-start | bytes 1572864 | tf_op jit(solution)/shard_map/all_to_all | solution.py:47
  118.2 5.0 %copy-start.9 = (f32[208,512]{1,0:T(8,128)S(1)}, f32[208,512]{1,0:T(8,128)}, u32[]{:S(2)}) copy-start(f32[208,512]{1,0:T(8,128)} %convert_element_type.63) | copy-start | bytes 1277956
  142.5 4.3 %collective-permute-start.5 = (f16[4,208,512]{2,1,0:T(8,128)(2,1)S(1)}, f16[4,208,512]{2,1,0:T(8,128)(2,1)S(1)}, u32[]{:S(2)}, u32[]{:S(2)}) collective-permute-start(f16[4,208,512]{2,1,0:T(8,128)(2,1)S(1)} %all_gather.12), channel_id=1, source_target_pairs={{0,32},{32,0},{1,33},{33,1},{2,34},{34,2},{3,35},{35,3},{4,36},{36... | collective-permute-start | bytes 2555912 | tf_op jit(solution)/shard_map/ppermute | solution.py:18
  147.1 1.9 copy-start.1
  147.1 2.9 %copy-start.2 = (f32[800,1024]{1,0:T(8,128)S(1)}, f32[800,1024]{1,0:T(8,128)}, u32[]{:S(2)}) copy-start(f32[800,1024]{1,0:T(8,128)} %get-tuple-element.29) | copy-start | bytes 9830404
  151.4 1.7 copy-start.11
  155.2 20.2 %all-to-all-start.3 = ((bf16[16,64,320]{2,1,0:T(8,128)(2,1)}), bf16[16,64,320]{2,1,0:T(8,128)(2,1)S(1)}, u32[]{:S(2)}, u32[]{:S(2)}) async-start(bf16[16,64,320]{2,1,0:T(8,128)(2,1)} %bitcast.27), calls=%async_computation.3 | async-start | bytes 1572864 | tf_op jit(solution)/shard_map/all_to_all | solution.py:138
  162.4 3.5 %copy-start.12 = (bf16[800,1024]{1,0:T(8,128)(2,1)S(1)}, bf16[800,1024]{1,0:T(8,128)(2,1)}, u32[]{:S(2)}) copy-start(bf16[800,1024]{1,0:T(8,128)(2,1)} %copy-done.11) | copy-start | bytes 4915204
  175.5 15.8 %collective-permute-start.6 = (f32[32,320]{1,0:T(8,128)S(1)}, f32[32,320]{1,0:T(8,128)S(1)}, u32[]{:S(2)}, u32[]{:S(2)}) collective-permute-start(f32[32,320]{1,0:T(8,128)S(1)} %slice.95), channel_id=1, source_target_pairs={{0,1},{1,0},{2,3},{3,2},{4,5},{5,4},{6,7},{7,6},{8,9},{9,8},{10,11... | collective-permute-start | bytes 122888 | tf_op jit(solution)/shard_map/ppermute | solution.py:18
  (4 other events, 5.4 us)
Sparse Core Ops, SparseCore 0:
  10.1 79.3 all-gather.2

commit v5 on v4

--- a/solution.py
+++ b/solution.py
@@ -130,17 +130,15 @@
 
     own, other = decode(coded)[0].reshape(800, 512), decode(coded_other)[0].reshape(800, 512)
     grad_hidden = by_core(own, other)
-    grad_gate = (grad_hidden * gate_slope).astype(BF16)
-    grad_up = (grad_hidden * silu_val).astype(BF16)
-
-    share = dot(grad_gate, gate_weight, 0, 1) + dot(grad_up, up_weight, 0, 1)
-    share = with_layout_constraint(share.astype(BF16), Layout(major_to_minor=(0, 1)))
+    grads = jnp.concatenate([grad_hidden * gate_slope, grad_hidden * silu_val]).astype(BF16)
+    share = dot(grads, jnp.concatenate([gate_weight, up_weight], axis=1), 0, 1).astype(BF16)
+    share = with_layout_constraint(share, Layout(major_to_minor=(0, 1)))
     share = lax.all_to_all(share.reshape(16, 64, 320), PLANE, 0, 0, tiled=True)
     share = jnp.sum(share.astype(F32), axis=0)
     grad_input = share[:32] + swap(share[32:], "h")
 
-    grad_gate_weight = dot(act_rows, grad_gate, 0, 1)
-    grad_up_weight = dot(act_rows, grad_up, 0, 1)
+    grad_gate_weight = dot(act_rows, grads[:800], 0, 1)
+    grad_up_weight = dot(act_rows, grads[800:], 0, 1)
     return (grad_input, grad_gate_weight, grad_up_weight, grad_down_weight)
 
 

time: 200 us -> 198 us (0.990)
  matrix products: 16.1 us -> 13.9 us
  other arithmetic: 17.5 us -> 19.5 us
    dot_general x7 -> x6, matrix products: 16.1 us -> 13.9 us  [dot(): lax.dot_general(left, right, (((of_left,), (of_right,)), ((), ())), prefe...]
  transfers between devices with their start and end apart: 12 -> 12, of which waited for: 7 -> 8; matrix products, arithmetic and copies ran while one was open for 19% -> 18% of each run, Pallas kernels for 0% -> 0%
where the time goes in v5:
time: 198 us; the launch traced here: 197 us
  starting transfers between devices  61.4 us (31%)
  waiting for transfers between devices  51.3 us (26%)
  blocking collectives  19.7 us (10%)
  other arithmetic  19.5 us (10%)
  between operations  14.4 us (7%)
  local copies, waits for them, and re-layouts  14.1 us (7%)
  matrix products  13.9 us (7%)
  loops' own time  2.81 us (1%)
    ppermute x7, starting transfers between devices, swap(): return lax.ppermute(x, axis, [(0, 1), (1, 0)])  38.6 us
    all_gather x1, waiting for transfers between devices, shards(): saved = lax.all_gather(saved, LINE, axis=0, tiled=False)  24.6 us
    all_gather x1, blocking collectives, shards(): coded = lax.all_gather(coded, QUAD, axis=0, tiled=False)  19.7 us
    all_to_all x2, starting transfers between devices, plane_gather(): lax.all_to_all(jnp.broadcast_to(x[None], (16,) + x.shape), PLANE, 0, 0, t...  14 us
    dot_general x6, matrix products, dot(): lax.dot_general(left, right, (((of_left,), (of_right,)), ((), ())), prefe...  13.9 us
    all_to_all x2, waiting for transfers between devices, plane_gather(): lax.all_to_all(jnp.broadcast_to(x[None], (16,) + x.shape), PLANE, 0, 0, t...  11.9 us
    all_to_all x1, waiting for transfers between devices, shards(): share = lax.all_to_all(share.reshape(16, 64, 320), PLANE, 0, 0, tiled=True)  7.68 us
    all_to_all x1, starting transfers between devices, shards(): share = lax.all_to_all(share.reshape(16, 64, 320), PLANE, 0, 0, tiled=True)  5.26 us
  transfers between devices with their start and end apart: 12, of which 8 were waited for; matrix products, arithmetic and copies ran while one was open for 18% of the time, Pallas kernels for 0%

profile of v5, /device:TPU:4, one launch (start us, length us, event | category | flops | bytes accessed | tf_op | source)
XLA Modules:
  0.0 197.2 jit_solution(16507097699028456774)
XLA Ops:
  9.0 51.9 %conditional.1 = (f16[4,208,512]{2,1,0:T(8,128)(2,1)}, bf16[1024,320]{1,0:T(8,128)(2,1)S(1)}, bf16[64,320]{1,0:T(8,128)(2,1)}) conditional(s32[]{:T(128)} %convert_element_type.56, () %tuple.18, (bf16[32,320]{1,0:T(8,128)(2,1)}, bf16[32,320]{1,0:T(8,128)(2,1)}, bf16[800,320]{0,1:T(8,128)(2,1)}) %tuple.19), branch_computations={%region_0.1_spmd, %region_1.6_spmd} | conditional | flops 549810368 | bytes 29340656 | solution.py:82
  9.8 15.7 %collective-permute-start = (bf16[2,32,320]{2,1,0:T(8,128)(2,1)S(1)}, bf16[2,32,320]{2,1,0:T(8,128)(2,1)S(1)}, u32[]{:S(2)}, u32[]{:S(2)}) collective-permute-start(bf16[2,32,320]{2,1,0:T(8,128)(2,1)S(1)} %pad_maximum_fusion.1), channel_id=1, source_target_pairs={{0,1},{1,0},{2,3},{3,2},{4,5},{5,4},{6,7},{7,6},{8,9},{9,8},{10,11... | collective-permute-start | bytes 122888 | tf_op jit(solution)/shard_map/cond/branch_1_fun/ppermute | solution.py:18
  28.1 1.9 collective-permute-start.2
  31.6 7.4 %all-to-all-start = ((bf16[16,64,320]{2,1,0:T(8,128)(2,1)}), bf16[16,64,320]{2,1,0:T(8,128)(2,1)S(1)}, u32[]{:S(2)}, u32[]{:S(2)}) async-start(bf16[16,64,320]{2,1,0:T(8,128)(2,1)} %broadcast_in_dim.12), calls=%async_computation | async-start | bytes 1572864 | tf_op jit(solution)/shard_map/cond/branch_1_fun/all_to_all | solution.py:47
  41.1 11.1 %all-to-all-done = bf16[16,64,320]{2,1,0:T(8,128)(2,1)S(1)} async-done(((bf16[16,64,320]{2,1,0:T(8,128)(2,1)}), bf16[16,64,320]{2,1,0:T(8,128)(2,1)S(1)}, u32[]{:S(2)}, u32[]{:S(2)}) %all-to-all-start) | async-done | bytes 655392 | tf_op jit(solution)/shard_map/cond/branch_1_fun/all_to_all | solution.py:47
  52.3 1.9 collective-permute-start.1
  60.9 3.5 %all-to-all-start.1 = ((f16[4,208,512]{2,1,0:T(8,128)(2,1)}), f16[4,208,512]{2,1,0:T(8,128)(2,1)S(1)}, u32[]{:S(2)}, u32[]{:S(2)}) async-start(f16[4,208,512]{2,1,0:T(8,128)(2,1)} %get-tuple-element.23), calls=%async_computation.1 | async-start | bytes 1703936 | tf_op jit(solution)/shard_map/all_to_all | solution.py:96
  64.4 24.6 %all-gather.3.cloned.1.call-done = bf16[1024,896]{1,0:T(8,128)(2,1)} async-done(((bf16[128,896]{1,0:T(8,128)(2,1)}), bf16[1024,896]{1,0:T(8,128)(2,1)}) %all-gather.3.cloned.1.call-update) | async-done | bytes 1835024 | tf_op jit(solution)/shard_map/all_gather | solution.py:81
  89.0 1.9 collective-permute-start.4
  90.9 3.3 %all-to-all-done.1 = f16[4,208,512]{2,1,0:T(8,128)(2,1)S(1)} async-done(((f16[4,208,512]{2,1,0:T(8,128)(2,1)}), f16[4,208,512]{2,1,0:T(8,128)(2,1)S(1)}, u32[]{:S(2)}, u32[]{:S(2)}) %all-to-all-start.1) | async-done | bytes 852000 | tf_op jit(solution)/shard_map/all_to_all | solution.py:96
  95.5 5.3 %collective-permute-start.3 = (f16[208,512]{1,0:T(8,128)(2,1)}, f16[208,512]{1,0:T(8,128)(2,1)}, u32[]{:S(2)}, u32[]{:S(2)}) collective-permute-start(f16[208,512]{1,0:T(8,128)(2,1)} %pad_maximum_fusion.6), channel_id=1, source_target_pairs={{0,256},{256,0},{1,257},{257,1},{2,258},{258,2},{3,259},{259,3},{4... | collective-permute-start | bytes 638984 | tf_op jit(solution)/shard_map/ppermute | solution.py:18
  102.6 1.8 broadcast_in_dim.28
  104.4 6.6 %all-to-all-start.2 = ((bf16[16,64,320]{2,1,0:T(8,128)(2,1)}), bf16[16,64,320]{2,1,0:T(8,128)(2,1)}, u32[]{:S(2)}, u32[]{:S(2)}) async-start(bf16[16,64,320]{2,1,0:T(8,128)(2,1)} %broadcast_in_dim.28), calls=%async_computation.2 | async-start | bytes 1572864 | tf_op jit(solution)/shard_map/all_to_all | solution.py:47
  118.9 3.2 %fusion.4 = (bf16[800,1024]{1,0:T(8,128)(2,1)}, f32[800,1024]{1,0:T(8,128)S(1)}, f32[800,1024]{1,0:T(8,128)}) fusion(bf16[800,512]{1,0:T(8,128)(2,1)S(1)} %get-tuple-element.68, bf16[800,512]{1,0:T(8,128)(2,1)S(1)} %get-tuple-element.67, bf16[800,512]{1,0:T(8,128)(2,1)S(1)} %get-tuple-element.75, bf16[800,512]{1,0:T(8,128)(2,1)S(1)} %get-tuple-element.76), kind=kLoop, calls=%fused_computation.21 | loop fusion | flops 15564800 | bytes 11468800 | tf_op jit(solution)/shard_map/convert_element_type | solution.py:117
  125.8 19.7 %all_gather.12 = f16[4,208,512]{2,1,0:T(8,128)(2,1)S(1)} all-gather(f16[1,208,512]{2,1,0:T(8,128)(2,1)S(1)} %pad_maximum_fusion.7), channel_id=1, replica_groups=mesh['p'=2,'q'=2,'r'=2,'c'=2,'y'=4,'v'=2,'w'=2,'h'=2] {'q','r'}, dimensions={0}, use_global_device_ids=true | all-gather | bytes 1064960 | tf_op jit(solution)/shard_map/all_gather | solution.py:126
  145.5 2.1 %collective-permute-start.5 = (f16[4,208,512]{2,1,0:T(8,128)(2,1)S(1)}, f16[4,208,512]{2,1,0:T(8,128)(2,1)S(1)}, u32[]{:S(2)}, u32[]{:S(2)}) collective-permute-start(f16[4,208,512]{2,1,0:T(8,128)(2,1)S(1)} %all_gather.12), channel_id=1, source_target_pairs={{0,32},{32,0},{1,33},{33,1},{2,34},{34,2},{3,35},{35,3},{4,36},{36... | collective-permute-start | bytes 2555912 | tf_op jit(solution)/shard_map/ppermute | solution.py:18
  147.9 1.9 collective-permute-done.5
  153.5 3.2 %fusion.16 = bf16[1024,320]{1,0:T(8,128)(2,1)} fusion(bf16[800,1024]{1,0:T(8,128)(2,1)S(1)} %get-tuple-element.57, bf16[800,1024]{1,0:T(8,128)(2,1)S(1)} %get-tuple-element.56, bf16[320,800]{1,0:T(8,128)(2,1)S(1)} %copy-done.14, bf16[320,800]{1,0:T(8,128)(2,1)S(1)} %copy-done.15), kind=kOutput, calls=%fused_computation.42 | convolution fusion | flops 1057505280 | bytes 4956160 | tf_op jit(solution)/shard_map/dot_general | solution.py:30
  156.7 5.3 %all-to-all-start.3 = ((bf16[16,64,320]{2,1,0:T(8,128)(2,1)}), bf16[16,64,320]{2,1,0:T(8,128)(2,1)S(1)}, u32[]{:S(2)}, u32[]{:S(2)}) async-start(bf16[16,64,320]{2,1,0:T(8,128)(2,1)} %bitcast.73), calls=%async_computation.3 | async-start | bytes 1572864 | tf_op jit(solution)/shard_map/all_to_all | solution.py:136
  162.0 1.9 fusion.35
  163.9 3.3 %fusion.33 = f32[320,800]{1,0:T(8,128)} fusion(bf16[1024,320]{1,0:T(8,128)(2,1)} %bitcast.9, bf16[800,1024]{1,0:T(8,128)(2,1)S(1)} %copy-done.10), kind=kOutput, calls=%fused_computation.83 | convolution fusion | flops 524288000 | bytes 3317760 | tf_op jit(solution)/shard_map/dot_general | solution.py:30
  167.2 7.7 %all-to-all-done.3 = bf16[16,64,320]{2,1,0:T(8,128)(2,1)S(1)} async-done(((bf16[16,64,320]{2,1,0:T(8,128)(2,1)}), bf16[16,64,320]{2,1,0:T(8,128)(2,1)S(1)}, u32[]{:S(2)}, u32[]{:S(2)}) %all-to-all-start.3) | async-done | bytes 655392 | tf_op jit(solution)/shard_map/all_to_all | solution.py:136
  175.0 9.8 %collective-permute-start.6 = (f32[32,320]{1,0:T(8,128)S(1)}, f32[32,320]{1,0:T(8,128)S(1)}, u32[]{:S(2)}, u32[]{:S(2)}) collective-permute-start(f32[32,320]{1,0:T(8,128)S(1)} %slice.103), channel_id=1, source_target_pairs={{0,1},{1,0},{2,3},{3,2},{4,5},{5,4},{6,7},{7,6},{8,9},{9,8},{10,11... | collective-permute-start | bytes 122888 | tf_op jit(solution)/shard_map/ppermute | solution.py:18
  184.8 3.2 %fusion.34 = f32[320,800]{1,0:T(8,128)} fusion(bf16[1024,320]{1,0:T(8,128)(2,1)} %bitcast.9, bf16[800,1024]{1,0:T(8,128)(2,1)S(1)} %copy-done.8), kind=kOutput, calls=%fused_computation.84 | convolution fusion | flops 524288000 | bytes 3317760 | tf_op jit(solution)/shard_map/dot_general | solution.py:30
  (92 shorter events, 33.7 us)
Async XLA Ops:
  7.2 81.8 %all-gather.3.cloned.1.call-start = ((), (), s32[]{:S(2)}) async-start(), calls=%async_computation.4 | async-start | bytes 2064384 | tf_op jit(solution)/shard_map/all_gather | solution.py:81
  9.8 20.2 %collective-permute-start = (bf16[2,32,320]{2,1,0:T(8,128)(2,1)S(1)}, bf16[2,32,320]{2,1,0:T(8,128)(2,1)S(1)}, u32[]{:S(2)}, u32[]{:S(2)}) collective-permute-start(bf16[2,32,320]{2,1,0:T(8,128)(2,1)S(1)} %pad_maximum_fusion.1), channel_id=1, source_target_pairs={{0,1},{1,0},{2,3},{3,2},{4,5},{5,4},{6,7},{7,6},{8,9},{9,8},{10,11... | collective-permute-start | bytes 122888 | tf_op jit(solution)/shard_map/cond/branch_1_fun/ppermute | solution.py:18
  25.5 4.5 %copy-start.12 = (bf16[32,320]{1,0:T(8,128)(2,1)S(1)}, bf16[32,320]{1,0:T(8,128)(2,1)}, u32[]{:S(2)}) copy-start(bf16[32,320]{1,0:T(8,128)(2,1)} %get-tuple-element.36) | copy-start | bytes 61444 | tf_op jit(solution)/shard_map/cond
  25.5 4.5 %copy-start.13 = (bf16[32,320]{1,0:T(8,128)(2,1)S(1)}, bf16[32,320]{1,0:T(8,128)(2,1)}, u32[]{:S(2)}) copy-start(bf16[32,320]{1,0:T(8,128)(2,1)} %get-tuple-element.37) | copy-start | bytes 61444 | tf_op jit(solution)/shard_map/cond
  28.1 11.1 %collective-permute-start.2 = (bf16[832,320]{0,1:T(8,128)(2,1)S(1)}, bf16[832,320]{0,1:T(8,128)(2,1)S(1)}, u32[]{:S(2)}, u32[]{:S(2)}) collective-permute-start(bf16[832,320]{0,1:T(8,128)(2,1)S(1)} %copy.25), channel_id=1, source_target_pairs={{0,32},{32,0},{1,33},{33,1},{2,34},{34,2},{3,35},{35,3},{4,36},{36... | collective-permute-start | bytes 1597448 | tf_op jit(solution)/shard_map/cond/branch_1_fun/ppermute | solution.py:18
  31.6 20.6 %all-to-all-start = ((bf16[16,64,320]{2,1,0:T(8,128)(2,1)}), bf16[16,64,320]{2,1,0:T(8,128)(2,1)S(1)}, u32[]{:S(2)}, u32[]{:S(2)}) async-start(bf16[16,64,320]{2,1,0:T(8,128)(2,1)} %broadcast_in_dim.12), calls=%async_computation | async-start | bytes 1572864 | tf_op jit(solution)/shard_map/cond/branch_1_fun/all_to_all | solution.py:47
  39.1 15.1 %copy-start.6 = (bf16[832,320]{0,1:T(8,128)(2,1)}, bf16[832,320]{0,1:T(8,128)(2,1)S(1)}, u32[]{:S(2)}) copy-start(bf16[832,320]{0,1:T(8,128)(2,1)S(1)} %collective-permute-done.2) | copy-start | bytes 1597444 | tf_op jit(solution)/shard_map/cond
  52.3 3.4 %copy-start.1 = (bf16[16,64,320]{2,1,0:T(8,128)(2,1)}, bf16[16,64,320]{2,1,0:T(8,128)(2,1)S(1)}, u32[]{:S(2)}) copy-start(bf16[16,64,320]{2,1,0:T(8,128)(2,1)S(1)} %all-to-all-done) | copy-start | bytes 1966084 | tf_op jit(solution)/shard_map/cond
  52.3 3.6 %collective-permute-start.1 = (bf16[512,320]{1,0:T(8,128)(2,1)S(1)}, bf16[512,320]{1,0:T(8,128)(2,1)S(1)}, u32[]{:S(2)}, u32[]{:S(2)}) collective-permute-start(bf16[512,320]{1,0:T(8,128)(2,1)S(1)} %constant_dynamic-slice_fusion), channel_id=1, source_target_pairs={{0,32},{32,0},{1,33},{33,1},{2,34},{34,2},{3,35},{35,3},{4,36},{36... | collective-permute-start | bytes 983048 | tf_op jit(solution)/shard_map/cond/branch_1_fun/ppermute | solution.py:18
  60.9 33.5 %copy-start.3 = (bf16[1024,320]{1,0:T(8,128)(2,1)}, bf16[1024,320]{1,0:T(8,128)(2,1)S(1)}, u32[]{:S(2)}) copy-start(bf16[1024,320]{1,0:T(8,128)(2,1)S(1)} %get-tuple-element.32) | copy-start | bytes 1966084
  60.9 33.3 %all-to-all-start.1 = ((f16[4,208,512]{2,1,0:T(8,128)(2,1)}), f16[4,208,512]{2,1,0:T(8,128)(2,1)S(1)}, u32[]{:S(2)}, u32[]{:S(2)}) async-start(f16[4,208,512]{2,1,0:T(8,128)(2,1)} %get-tuple-element.23), calls=%async_computation.1 | async-start | bytes 1703936 | tf_op jit(solution)/shard_map/all_to_all | solution.py:96
  89.0 24.5 %collective-permute-start.4 = (bf16[8,128,896]{2,1,0:T(8,128)(2,1)}, bf16[8,128,896]{2,1,0:T(8,128)(2,1)}, u32[]{:S(2)}, u32[]{:S(2)}) collective-permute-start(bf16[8,128,896]{2,1,0:T(8,128)(2,1)} %bitcast.70), channel_id=1, source_target_pairs={{0,32},{32,0},{1,33},{33,1},{2,34},{34,2},{3,35},{35,3},{4,36},{36... | collective-permute-start | bytes 5505032 | tf_op jit(solution)/shard_map/ppermute | solution.py:18
  95.5 26.6 %collective-permute-start.3 = (f16[208,512]{1,0:T(8,128)(2,1)}, f16[208,512]{1,0:T(8,128)(2,1)}, u32[]{:S(2)}, u32[]{:S(2)}) collective-permute-start(f16[208,512]{1,0:T(8,128)(2,1)} %pad_maximum_fusion.6), channel_id=1, source_target_pairs={{0,256},{256,0},{1,257},{257,1},{2,258},{258,2},{3,259},{259,3},{4... | collective-permute-start | bytes 638984 | tf_op jit(solution)/shard_map/ppermute | solution.py:18
  104.4 18.6 %all-to-all-start.2 = ((bf16[16,64,320]{2,1,0:T(8,128)(2,1)}), bf16[16,64,320]{2,1,0:T(8,128)(2,1)}, u32[]{:S(2)}, u32[]{:S(2)}) async-start(bf16[16,64,320]{2,1,0:T(8,128)(2,1)} %broadcast_in_dim.28), calls=%async_computation.2 | async-start | bytes 1572864 | tf_op jit(solution)/shard_map/all_to_all | solution.py:47
  145.5 4.3 %collective-permute-start.5 = (f16[4,208,512]{2,1,0:T(8,128)(2,1)S(1)}, f16[4,208,512]{2,1,0:T(8,128)(2,1)S(1)}, u32[]{:S(2)}, u32[]{:S(2)}) collective-permute-start(f16[4,208,512]{2,1,0:T(8,128)(2,1)S(1)} %all_gather.12), channel_id=1, source_target_pairs={{0,32},{32,0},{1,33},{33,1},{2,34},{34,2},{3,35},{35,3},{4,36},{36... | collective-permute-start | bytes 2555912 | tf_op jit(solution)/shard_map/ppermute | solution.py:18
  150.1 1.9 copy-start
  153.4 3.3 %copy-start.7 = (bf16[800,1024]{1,0:T(8,128)(2,1)}, bf16[800,1024]{1,0:T(8,128)(2,1)S(1)}, u32[]{:S(2)}) copy-start(bf16[800,1024]{1,0:T(8,128)(2,1)S(1)} %get-tuple-element.57) | copy-start | bytes 4915204
  153.4 3.3 %copy-start.9 = (bf16[800,1024]{1,0:T(8,128)(2,1)}, bf16[800,1024]{1,0:T(8,128)(2,1)S(1)}, u32[]{:S(2)}) copy-start(bf16[800,1024]{1,0:T(8,128)(2,1)S(1)} %get-tuple-element.56) | copy-start | bytes 4915204
  153.4 8.5 %copy-start.4 = (bf16[1024,320]{1,0:T(8,128)(2,1)S(1)}, bf16[1024,320]{1,0:T(8,128)(2,1)}, u32[]{:S(2)}) copy-start(bf16[1024,320]{1,0:T(8,128)(2,1)} %copy-done.3) | copy-start | bytes 1966084
  153.4 8.5 %copy-start.11 = (bf16[800,1024]{1,0:T(8,128)(2,1)S(1)}, bf16[800,1024]{1,0:T(8,128)(2,1)}, u32[]{:S(2)}) copy-start(bf16[800,1024]{1,0:T(8,128)(2,1)} %get-tuple-element.31) | copy-start | bytes 4915204
  156.7 18.2 %all-to-all-start.3 = ((bf16[16,64,320]{2,1,0:T(8,128)(2,1)}), bf16[16,64,320]{2,1,0:T(8,128)(2,1)S(1)}, u32[]{:S(2)}, u32[]{:S(2)}) async-start(bf16[16,64,320]{2,1,0:T(8,128)(2,1)} %bitcast.73), calls=%async_computation.3 | async-start | bytes 1572864 | tf_op jit(solution)/shard_map/all_to_all | solution.py:136
  161.9 1.9 copy-start.10
  163.9 20.9 %copy-start.8 = (bf16[800,1024]{1,0:T(8,128)(2,1)S(1)}, bf16[800,1024]{1,0:T(8,128)(2,1)}, u32[]{:S(2)}) copy-start(bf16[800,1024]{1,0:T(8,128)(2,1)} %copy-done.7) | copy-start | bytes 4915204
  175.0 14.7 %collective-permute-start.6 = (f32[32,320]{1,0:T(8,128)S(1)}, f32[32,320]{1,0:T(8,128)S(1)}, u32[]{:S(2)}, u32[]{:S(2)}) collective-permute-start(f32[32,320]{1,0:T(8,128)S(1)} %slice.103), channel_id=1, source_target_pairs={{0,1},{1,0},{2,3},{3,2},{4,5},{5,4},{6,7},{7,6},{8,9},{9,8},{10,11... | collective-permute-start | bytes 122888 | tf_op jit(solution)/shard_map/ppermute | solution.py:18
  (4 other events, 5.2 us)
Sparse Core Ops, SparseCore 0:
  10.1 78.8 all-gather.2
